TPU v7x, 512 devices: a whole 4x4x16 slice. The times are simulated.
512 devices in a mesh: row: 16 (over z), col: 32 (over x, y, core).
Axes of the slice: x: 4, y: 4, z: 16, core: 2. Of those that a mesh axis runs over, the one named last changes fastest.
Arguments:
- heights: int32 [1024, 2048], P('row', 'col'), may hold values from 0 to 199
- blocked: int32 [1024, 2048], P('row', 'col'), may hold values 0 or 1
- estimate: bfloat16 [1024, 65536], P('row', 'col'), may hold values from 0 to 48
- portal_index: int32 [16, 32, 32], P('row', 'col'), may hold values from 0 to 4095, as said below
Outputs:
- relaxed: bfloat16 [1024, 65536], P('row', 'col')
- merged: float32 [16, 32, 32, 32], P('row', 'col')
Inputs may be any that keep to these rules, and one draw needn't show every extreme that they name: `portal_index`: the 32 portal cells of a tile are all different.
All inputs are finite; a program needn't handle non-finite values. No bound on the sum of `blocked` on one device may be relied on, other than what follows from the above.
Results may differ from a plain program's by a relative error of at most 0.001.
Values sent between devices are 32-bit elements; how exact they have to be, the bound alone decides.
A program may use at most 128 MiB of HBM per device.

v0:
```python
import jax
import jax.numpy as jnp
from jax import lax
from jax.sharding import PartitionSpec as P

SWEEPS = 8
LEVELS = 2


far_value = 1000000.0


def with_halo(block, sides, width):
    for axis, dim in sides:
        count = lax.axis_size(axis)
        forward = [(i, i + 1) for i in range(count - 1)]
        backward = [(target, source) for source, target in forward]
        low = lax.ppermute(
            lax.slice_in_dim(block, block.shape[dim] - width, None, axis=dim), axis, forward
        )
        high = lax.ppermute(lax.slice_in_dim(block, 0, width, axis=dim), axis, backward)
        block = jnp.concatenate([low, block, high], axis=dim)
    return block


def swapped(block, axis, bit):
    count = lax.axis_size(axis)
    route = []
    for low in range(count):
        high = low | 1 << bit
        if high != low and high < count:
            route += [(low, high), (high, low)]
    return lax.ppermute(block, axis, route)


def slope_cost(padded_heights, blocked):
    grad_x = (padded_heights[1:-1, 2:] - padded_heights[1:-1, :-2]).astype(jnp.float32) * 0.01
    grad_y = (padded_heights[2:, 1:-1] - padded_heights[:-2, 1:-1]).astype(jnp.float32) * 0.01
    grad_sq = grad_x * grad_x + grad_y * grad_y
    return (
        1.0
        + 2.0 * grad_sq
        + 0.5 * grad_y / jnp.sqrt(1.0 + grad_sq)
        + 30.0 * blocked.astype(jnp.float32)
    )


def relax_flat(extended, cost_rep, portals):
    centre_cost = cost_rep[1:-1, portals:-portals]
    centre_cells = extended[1:-1, portals:-portals]
    north = extended[:-2, portals:-portals] + 0.5 * (centre_cost + cost_rep[:-2, portals:-portals])
    south = extended[2:, portals:-portals] + 0.5 * (centre_cost + cost_rep[2:, portals:-portals])
    west = extended[1:-1, : -2 * portals] + 0.5 * (centre_cost + cost_rep[1:-1, : -2 * portals])
    east = extended[1:-1, 2 * portals :] + 0.5 * (centre_cost + cost_rep[1:-1, 2 * portals :])
    nearest = jnp.minimum(jnp.minimum(north, south), jnp.minimum(west, east))
    return jnp.minimum(centre_cells, nearest)


def minplus(left, right):
    return jnp.min(left[..., :, :, None] + right[..., None, :, :], axis=-2)


def merge_pair(table_now, partner):
    return jnp.minimum(table_now, minplus(minplus(table_now, partner), table_now))


def inside_mask(row_index, col_index, tile_side, row_count, col_count, margin, portals):
    span = jnp.arange(-margin, tile_side + margin, dtype=jnp.int32)
    global_rows = row_index * tile_side + span
    global_cols = col_index * tile_side + span
    inside_rows = (global_rows >= 0) & (global_rows < row_count * tile_side)
    inside_cols = (global_cols >= 0) & (global_cols < col_count * tile_side)
    inside_cols = jnp.repeat(inside_cols, portals)
    return inside_rows[:, None] & inside_cols[None, :]


def body(heights, blocked, estimate, portal_index):
    tile_side = heights.shape[0]
    portals = estimate.shape[1] // tile_side
    row_index = lax.axis_index("row")
    col_index = lax.axis_index("col")
    row_count = lax.axis_size("row")
    col_count = lax.axis_size("col")
    heights_ext = with_halo(heights, (("row", 0), ("col", 1)), 1)
    heights_ext = heights_ext.at[0].set(jnp.where(row_index == 0, heights_ext[1], heights_ext[0]))
    heights_ext = heights_ext.at[-1].set(
        jnp.where(row_index == row_count - 1, heights_ext[-2], heights_ext[-1])
    )
    heights_ext = heights_ext.at[:, 0].set(
        jnp.where(col_index == 0, heights_ext[:, 1], heights_ext[:, 0])
    )
    heights_ext = heights_ext.at[:, -1].set(
        jnp.where(col_index == col_count - 1, heights_ext[:, -2], heights_ext[:, -1])
    )
    step_cost = slope_cost(heights_ext, blocked)
    portal_cells = portal_index[0, 0]
    cell_row = portal_cells // tile_side
    cell_col = portal_cells % tile_side
    class_ids = jnp.arange(portals, dtype=jnp.int32)
    dist_field = estimate.astype(jnp.float32)
    dist_field = dist_field.at[cell_row, cell_col * portals + class_ids].set(0.0)
    rim_depth = 1
    cost_ext = with_halo(step_cost, (("row", 0), ("col", 1)), rim_depth)
    cost_rep = jnp.repeat(cost_ext, portals, axis=1)
    margin_masks = inside_mask(
        row_index, col_index, tile_side, row_count, col_count, rim_depth, portals
    )
    for outer_step in range(SWEEPS // rim_depth):
        wider = with_halo(dist_field, (("col", 1),), rim_depth * portals)
        extended = with_halo(wider, (("row", 0),), rim_depth)
        extended = jnp.where(margin_masks, extended, far_value)
        extended = relax_flat(extended, cost_rep, portals)
        dist_field = extended
    table_now = dist_field.reshape(tile_side, tile_side, portals)[cell_row, cell_col]
    for level in range(LEVELS):
        partner = swapped(table_now, "row", level)
        table_now = merge_pair(table_now, partner)
        partner = swapped(table_now, "col", level)
        table_now = merge_pair(table_now, partner)
    return (dist_field.astype(jnp.bfloat16), (table_now * 0.0625)[None, None])


def solution(mesh):
    placed = (P("row", "col"), P("row", "col"), P("row", "col"), P("row", "col", None))
    return jax.shard_map(
        body,
        mesh=mesh,
        in_specs=placed,
        out_specs=(P("row", "col"), P("row", "col", None, None)),
        check_vma=False,
    )
```

profile of v0, /device:TPU:4, one launch (start us, length us, event | category | flops | bytes accessed | tf_op | source)
XLA Modules:
  0.0 241.0 jit_solution(3392481338313548059)
XLA Ops:
  1.4 3.8 %collective-permute-start.4 = (s32[1,64]{1,0:T(1,128)S(1)}, s32[1,64]{1,0:T(1,128)S(1)}, u32[]{:S(2)}, u32[]{:S(2)}) collective-permute-start(s32[1,64]{1,0:T(1,128)S(1)} %get-tuple-element.103), channel_id=1, source_target_pairs={{0,32},{32,64},{64,96},{96,128},{128,160},{160,192},{192,224},{224... | collective-permute-start | bytes 776 | tf_op jit(solution)/shard_map/ppermute | solution.py:18
  8.2 2.2 scatter_fusion
  10.4 1.9 collective-permute-start
  12.4 5.8 %collective-permute-start.1 = (f32[64,32]{1,0:T(8,128)S(1)}, f32[64,32]{1,0:T(8,128)S(1)}, u32[]{:S(2)}, u32[]{:S(2)}) collective-permute-start(f32[64,32]{1,0:T(8,128)S(1)} %get-tuple-element.95), channel_id=1, source_target_pairs={{1,0},{2,1},{3,2},{4,3},{5,4},{6,5},{7,6},{8,7},{9,8},{10,9},{11,1... | collective-permute-start | bytes 24584 | tf_op jit(solution)/shard_map/ppermute | solution.py:21
  19.0 1.9 collective-permute-start.6
  20.9 5.8 %collective-permute-start.7 = (s32[66,1]{1,0:T(8,128)S(1)}, s32[66,1]{1,0:T(8,128)S(1)}, u32[]{:S(2)}, u32[]{:S(2)}) collective-permute-start(s32[66,1]{1,0:T(8,128)S(1)} %get-tuple-element.100), channel_id=1, source_target_pairs={{1,0},{2,1},{3,2},{4,3},{5,4},{6,5},{7,6},{8,7},{9,8},{10,9},{11,1... | collective-permute-start | bytes 800 | tf_op jit(solution)/shard_map/ppermute | solution.py:21
  29.9 4.5 %collective-permute-start.8 = (f32[1,64]{1,0:T(1,128)S(1)}, f32[1,64]{1,0:T(1,128)S(1)}, u32[]{:S(2)}, u32[]{:S(2)}) collective-permute-start(f32[1,64]{1,0:T(1,128)S(1)} %get-tuple-element.101), channel_id=1, source_target_pairs={{0,32},{32,64},{64,96},{96,128},{128,160},{160,192},{192,224},{224... | collective-permute-start | bytes 776 | tf_op jit(solution)/shard_map/ppermute | solution.py:18
  35.8 4.1 %collective-permute-done.9 = f32[1,64]{1,0:T(1,128)S(1)} collective-permute-done((f32[1,64]{1,0:T(1,128)S(1)}, f32[1,64]{1,0:T(1,128)S(1)}, u32[]{:S(2)}, u32[]{:S(2)}) %collective-permute-start.9) | collective-permute-done | bytes 288 | tf_op jit(solution)/shard_map/ppermute | solution.py:21
  40.0 1.9 collective-permute-start.10
  41.9 5.8 %collective-permute-start.11 = (f32[66,1]{1,0:T(8,128)S(1)}, f32[66,1]{1,0:T(8,128)S(1)}, u32[]{:S(2)}, u32[]{:S(2)}) collective-permute-start(f32[66,1]{1,0:T(8,128)S(1)} %get-tuple-element.98), channel_id=1, source_target_pairs={{1,0},{2,1},{3,2},{4,3},{5,4},{6,5},{7,6},{8,7},{9,8},{10,9},{11,1... | collective-permute-start | bytes 800 | tf_op jit(solution)/shard_map/ppermute | solution.py:21
  49.9 4.9 %collective-permute-start.2 = (f32[1,2112]{1,0:T(1,128)S(1)}, f32[1,2112]{1,0:T(1,128)S(1)}, u32[]{:S(2)}, u32[]{:S(2)}) collective-permute-start(f32[1,2112]{1,0:T(1,128)S(1)} %get-tuple-element.79), channel_id=1, source_target_pairs={{0,32},{32,64},{64,96},{96,128},{128,160},{160,192},{192,224},{224... | collective-permute-start | bytes 25352 | tf_op jit(solution)/shard_map/ppermute | solution.py:18
  56.1 2.5 %fusion.45 = (f32[64,2048]{0,1:T(8,128)S(1)}, f32[64,2048]{0,1:T(8,128)S(1)}, f32[64,2048]{0,1:T(8,128)S(1)}, f32[64,2048]{0,1:T(8,128)}, f32[64,2048]{0,1:T(8,128)}) fusion(f32[66,2112]{0,1:T(8,128)S(1)} %bitcast.23), kind=kLoop, calls=%fused_computation.126 | loop fusion | bytes 5242880 | tf_op jit(solution)/shard_map/slice | solution.py:54
  58.6 2.3 copy.22
  60.9 2.4 copy.23
  66.8 2.1 fusion.30
  71.0 5.8 %collective-permute-start.13 = (f32[64,32]{1,0:T(8,128)S(1)}, f32[64,32]{1,0:T(8,128)S(1)}, u32[]{:S(2)}, u32[]{:S(2)}) collective-permute-start(f32[64,32]{1,0:T(8,128)S(1)} %get-tuple-element.93), channel_id=1, source_target_pairs={{1,0},{2,1},{3,2},{4,3},{5,4},{6,5},{7,6},{8,7},{9,8},{10,9},{11,1... | collective-permute-start | bytes 24584 | tf_op jit(solution)/shard_map/ppermute | solution.py:21
  78.7 5.8 %collective-permute-start.14 = (f32[1,2112]{1,0:T(1,128)S(1)}, f32[1,2112]{1,0:T(1,128)S(1)}, u32[]{:S(2)}, u32[]{:S(2)}) collective-permute-start(f32[1,2112]{1,0:T(1,128)S(1)} %get-tuple-element.77), channel_id=1, source_target_pairs={{0,32},{32,64},{64,96},{96,128},{128,160},{160,192},{192,224},{224... | collective-permute-start | bytes 25352 | tf_op jit(solution)/shard_map/ppermute | solution.py:18
  85.8 5.4 %collective-permute-done.15 = f32[1,2112]{1,0:T(1,128)S(1)} collective-permute-done((f32[1,2112]{1,0:T(1,128)S(1)}, f32[1,2112]{1,0:T(1,128)S(1)}, u32[]{:S(2)}, u32[]{:S(2)}) %collective-permute-start.15) | collective-permute-done | bytes 8480 | tf_op jit(solution)/shard_map/ppermute | solution.py:21
  92.0 1.9 collective-permute-start.16
  94.0 5.8 %collective-permute-start.17 = (f32[64,32]{1,0:T(8,128)S(1)}, f32[64,32]{1,0:T(8,128)S(1)}, u32[]{:S(2)}, u32[]{:S(2)}) collective-permute-start(f32[64,32]{1,0:T(8,128)S(1)} %get-tuple-element.91), channel_id=1, source_target_pairs={{1,0},{2,1},{3,2},{4,3},{5,4},{6,5},{7,6},{8,7},{9,8},{10,9},{11,1... | collective-permute-start | bytes 24584 | tf_op jit(solution)/shard_map/ppermute | solution.py:21
  101.7 3.9 %collective-permute-start.18 = (f32[1,2112]{1,0:T(1,128)S(1)}, f32[1,2112]{1,0:T(1,128)S(1)}, u32[]{:S(2)}, u32[]{:S(2)}) collective-permute-start(f32[1,2112]{1,0:T(1,128)S(1)} %get-tuple-element.75), channel_id=1, source_target_pairs={{0,32},{32,64},{64,96},{96,128},{128,160},{160,192},{192,224},{224... | collective-permute-start | bytes 25352 | tf_op jit(solution)/shard_map/ppermute | solution.py:18
  106.9 4.2 %collective-permute-done.19 = f32[1,2112]{1,0:T(1,128)S(1)} collective-permute-done((f32[1,2112]{1,0:T(1,128)S(1)}, f32[1,2112]{1,0:T(1,128)S(1)}, u32[]{:S(2)}, u32[]{:S(2)}) %collective-permute-start.19) | collective-permute-done | bytes 8480 | tf_op jit(solution)/shard_map/ppermute | solution.py:21
  112.0 1.9 collective-permute-start.20
  113.9 5.8 %collective-permute-start.21 = (f32[64,32]{1,0:T(8,128)S(1)}, f32[64,32]{1,0:T(8,128)S(1)}, u32[]{:S(2)}, u32[]{:S(2)}) collective-permute-start(f32[64,32]{1,0:T(8,128)S(1)} %get-tuple-element.89), channel_id=1, source_target_pairs={{1,0},{2,1},{3,2},{4,3},{5,4},{6,5},{7,6},{8,7},{9,8},{10,9},{11,1... | collective-permute-start | bytes 24584 | tf_op jit(solution)/shard_map/ppermute | solution.py:21
  121.6 4.3 %collective-permute-start.22 = (f32[1,2112]{1,0:T(1,128)S(1)}, f32[1,2112]{1,0:T(1,128)S(1)}, u32[]{:S(2)}, u32[]{:S(2)}) collective-permute-start(f32[1,2112]{1,0:T(1,128)S(1)} %get-tuple-element.73), channel_id=1, source_target_pairs={{0,32},{32,64},{64,96},{96,128},{128,160},{160,192},{192,224},{224... | collective-permute-start | bytes 25352 | tf_op jit(solution)/shard_map/ppermute | solution.py:18
  127.3 4.6 %collective-permute-done.23 = f32[1,2112]{1,0:T(1,128)S(1)} collective-permute-done((f32[1,2112]{1,0:T(1,128)S(1)}, f32[1,2112]{1,0:T(1,128)S(1)}, u32[]{:S(2)}, u32[]{:S(2)}) %collective-permute-start.23) | collective-permute-done | bytes 8480 | tf_op jit(solution)/shard_map/ppermute | solution.py:21
  132.8 1.9 collective-permute-start.24
  134.7 5.8 %collective-permute-start.25 = (f32[64,32]{1,0:T(8,128)S(1)}, f32[64,32]{1,0:T(8,128)S(1)}, u32[]{:S(2)}, u32[]{:S(2)}) collective-permute-start(f32[64,32]{1,0:T(8,128)S(1)} %get-tuple-element.87), channel_id=1, source_target_pairs={{1,0},{2,1},{3,2},{4,3},{5,4},{6,5},{7,6},{8,7},{9,8},{10,9},{11,1... | collective-permute-start | bytes 24584 | tf_op jit(solution)/shard_map/ppermute | solution.py:21
  142.4 5.1 %collective-permute-start.26 = (f32[1,2112]{1,0:T(1,128)S(1)}, f32[1,2112]{1,0:T(1,128)S(1)}, u32[]{:S(2)}, u32[]{:S(2)}) collective-permute-start(f32[1,2112]{1,0:T(1,128)S(1)} %get-tuple-element.71), channel_id=1, source_target_pairs={{0,32},{32,64},{64,96},{96,128},{128,160},{160,192},{192,224},{224... | collective-permute-start | bytes 25352 | tf_op jit(solution)/shard_map/ppermute | solution.py:18
  148.9 4.2 %collective-permute-done.27 = f32[1,2112]{1,0:T(1,128)S(1)} collective-permute-done((f32[1,2112]{1,0:T(1,128)S(1)}, f32[1,2112]{1,0:T(1,128)S(1)}, u32[]{:S(2)}, u32[]{:S(2)}) %collective-permute-start.27) | collective-permute-done | bytes 8480 | tf_op jit(solution)/shard_map/ppermute | solution.py:21
  153.9 1.9 collective-permute-start.28
  155.9 5.8 %collective-permute-start.29 = (f32[64,32]{1,0:T(8,128)S(1)}, f32[64,32]{1,0:T(8,128)S(1)}, u32[]{:S(2)}, u32[]{:S(2)}) collective-permute-start(f32[64,32]{1,0:T(8,128)S(1)} %get-tuple-element.85), channel_id=1, source_target_pairs={{1,0},{2,1},{3,2},{4,3},{5,4},{6,5},{7,6},{8,7},{9,8},{10,9},{11,1... | collective-permute-start | bytes 24584 | tf_op jit(solution)/shard_map/ppermute | solution.py:21
  163.5 3.9 %collective-permute-start.30 = (f32[1,2112]{1,0:T(1,128)S(1)}, f32[1,2112]{1,0:T(1,128)S(1)}, u32[]{:S(2)}, u32[]{:S(2)}) collective-permute-start(f32[1,2112]{1,0:T(1,128)S(1)} %get-tuple-element.69), channel_id=1, source_target_pairs={{0,32},{32,64},{64,96},{96,128},{128,160},{160,192},{192,224},{224... | collective-permute-start | bytes 25352 | tf_op jit(solution)/shard_map/ppermute | solution.py:18
  169.0 4.1 %collective-permute-done.31 = f32[1,2112]{1,0:T(1,128)S(1)} collective-permute-done((f32[1,2112]{1,0:T(1,128)S(1)}, f32[1,2112]{1,0:T(1,128)S(1)}, u32[]{:S(2)}, u32[]{:S(2)}) %collective-permute-start.31) | collective-permute-done | bytes 8480 | tf_op jit(solution)/shard_map/ppermute | solution.py:21
  173.9 1.9 collective-permute-start.32
  175.8 5.8 %collective-permute-start.33 = (f32[64,32]{1,0:T(8,128)S(1)}, f32[64,32]{1,0:T(8,128)S(1)}, u32[]{:S(2)}, u32[]{:S(2)}) collective-permute-start(f32[64,32]{1,0:T(8,128)S(1)} %get-tuple-element.83), channel_id=1, source_target_pairs={{1,0},{2,1},{3,2},{4,3},{5,4},{6,5},{7,6},{8,7},{9,8},{10,9},{11,1... | collective-permute-start | bytes 24584 | tf_op jit(solution)/shard_map/ppermute | solution.py:21
  183.5 4.3 %collective-permute-start.34 = (f32[1,2112]{1,0:T(1,128)S(1)}, f32[1,2112]{1,0:T(1,128)S(1)}, u32[]{:S(2)}, u32[]{:S(2)}) collective-permute-start(f32[1,2112]{1,0:T(1,128)S(1)} %get-tuple-element.67), channel_id=1, source_target_pairs={{0,32},{32,64},{64,96},{96,128},{128,160},{160,192},{192,224},{224... | collective-permute-start | bytes 25352 | tf_op jit(solution)/shard_map/ppermute | solution.py:18
  189.2 4.2 %collective-permute-done.35 = f32[1,2112]{1,0:T(1,128)S(1)} collective-permute-done((f32[1,2112]{1,0:T(1,128)S(1)}, f32[1,2112]{1,0:T(1,128)S(1)}, u32[]{:S(2)}, u32[]{:S(2)}) %collective-permute-start.35) | collective-permute-done | bytes 8480 | tf_op jit(solution)/shard_map/ppermute | solution.py:21
  194.3 1.9 collective-permute-start.36
  196.2 5.8 %collective-permute-start.37 = (f32[64,32]{1,0:T(8,128)S(1)}, f32[64,32]{1,0:T(8,128)S(1)}, u32[]{:S(2)}, u32[]{:S(2)}) collective-permute-start(f32[64,32]{1,0:T(8,128)S(1)} %get-tuple-element.81), channel_id=1, source_target_pairs={{1,0},{2,1},{3,2},{4,3},{5,4},{6,5},{7,6},{8,7},{9,8},{10,9},{11,1... | collective-permute-start | bytes 24584 | tf_op jit(solution)/shard_map/ppermute | solution.py:21
  203.9 3.9 %collective-permute-start.38 = (f32[1,2112]{1,0:T(1,128)S(1)}, f32[1,2112]{1,0:T(1,128)S(1)}, u32[]{:S(2)}, u32[]{:S(2)}) collective-permute-start(f32[1,2112]{1,0:T(1,128)S(1)} %get-tuple-element.65), channel_id=1, source_target_pairs={{0,32},{32,64},{64,96},{96,128},{128,160},{160,192},{192,224},{224... | collective-permute-start | bytes 25352 | tf_op jit(solution)/shard_map/ppermute | solution.py:18
  209.1 4.2 %collective-permute-done.39 = f32[1,2112]{1,0:T(1,128)S(1)} collective-permute-done((f32[1,2112]{1,0:T(1,128)S(1)}, f32[1,2112]{1,0:T(1,128)S(1)}, u32[]{:S(2)}, u32[]{:S(2)}) %collective-permute-start.39) | collective-permute-done | bytes 8480 | tf_op jit(solution)/shard_map/ppermute | solution.py:21
  217.7 3.9 %collective-permute-start.40 = (f32[32,32]{1,0:T(8,128)S(1)}, f32[32,32]{1,0:T(8,128)S(1)}, u32[]{:S(2)}, u32[]{:S(2)}) collective-permute-start(f32[32,32]{1,0:T(8,128)S(1)} %gather_fusion), channel_id=1, source_target_pairs={{0,32},{32,0},{64,96},{96,64},{128,160},{160,128},{192,224},{224,1... | collective-permute-start | bytes 12296 | tf_op jit(solution)/shard_map/ppermute | solution.py:33
  223.8 1.9 collective-permute-start.41
  227.3 4.6 %collective-permute-start.42 = (f32[32,32]{1,0:T(8,128)S(1)}, f32[32,32]{1,0:T(8,128)S(1)}, u32[]{:S(2)}, u32[]{:S(2)}) collective-permute-start(f32[32,32]{1,0:T(8,128)S(1)} %min.217), channel_id=1, source_target_pairs={{0,64},{64,0},{32,96},{96,32},{128,192},{192,128},{160,224},{224,1... | collective-permute-start | bytes 12296 | tf_op jit(solution)/shard_map/ppermute | solution.py:33
  231.9 1.9 collective-permute-done.42
  234.3 1.9 collective-permute-start.43
  236.3 3.7 %collective-permute-done.43 = f32[32,32]{1,0:T(8,128)S(1)} collective-permute-done((f32[32,32]{1,0:T(8,128)S(1)}, f32[32,32]{1,0:T(8,128)S(1)}, u32[]{:S(2)}, u32[]{:S(2)}) %collective-permute-start.43) | collective-permute-done | bytes 4128 | tf_op jit(solution)/shard_map/ppermute | solution.py:33
  (140 shorter events, 55.8 us)
Async XLA Ops:
  0.6 27.7 %copy-start.3 = (s32[64,64]{1,0:T(8,128)S(1)}, s32[64,64]{1,0:T(8,128)}, u32[]{:S(2)}) copy-start(s32[64,64]{1,0:T(8,128)} %param.12) | copy-start | bytes 49156
  0.6 29.2 %copy-start.4 = (s32[64,64]{1,0:T(8,128)S(1)}, s32[64,64]{1,0:T(8,128)}, u32[]{:S(2)}) copy-start(s32[64,64]{1,0:T(8,128)} %param.13) | copy-start | bytes 49156
  1.4 16.7 %collective-permute-start.4 = (s32[1,64]{1,0:T(1,128)S(1)}, s32[1,64]{1,0:T(1,128)S(1)}, u32[]{:S(2)}, u32[]{:S(2)}) collective-permute-start(s32[1,64]{1,0:T(1,128)S(1)} %get-tuple-element.103), channel_id=1, source_target_pairs={{0,32},{32,64},{64,96},{96,128},{128,160},{160,192},{192,224},{224... | collective-permute-start | bytes 776 | tf_op jit(solution)/shard_map/ppermute | solution.py:18
  5.2 12.9 %collective-permute-start.5 = (s32[1,64]{1,0:T(1,128)S(1)}, s32[1,64]{1,0:T(1,128)S(1)}, u32[]{:S(2)}, u32[]{:S(2)}) collective-permute-start(s32[1,64]{1,0:T(1,128)S(1)} %get-tuple-element.104), channel_id=1, source_target_pairs={{32,0},{64,32},{96,64},{128,96},{160,128},{192,160},{224,192},{256... | collective-permute-start | bytes 776 | tf_op jit(solution)/shard_map/ppermute | solution.py:21
  10.4 39.0 %collective-permute-start = (f32[64,32]{1,0:T(8,128)S(1)}, f32[64,32]{1,0:T(8,128)S(1)}, u32[]{:S(2)}, u32[]{:S(2)}) collective-permute-start(f32[64,32]{1,0:T(8,128)S(1)} %get-tuple-element.96), channel_id=1, source_target_pairs={{0,1},{1,2},{2,3},{3,4},{4,5},{5,6},{6,7},{7,8},{8,9},{9,10},{10,1... | collective-permute-start | bytes 24584 | tf_op jit(solution)/shard_map/ppermute | solution.py:18
  12.4 37.1 %collective-permute-start.1 = (f32[64,32]{1,0:T(8,128)S(1)}, f32[64,32]{1,0:T(8,128)S(1)}, u32[]{:S(2)}, u32[]{:S(2)}) collective-permute-start(f32[64,32]{1,0:T(8,128)S(1)} %get-tuple-element.95), channel_id=1, source_target_pairs={{1,0},{2,1},{3,2},{4,3},{5,4},{6,5},{7,6},{8,7},{9,8},{10,9},{11,1... | collective-permute-start | bytes 24584 | tf_op jit(solution)/shard_map/ppermute | solution.py:21
  19.0 8.3 %collective-permute-start.6 = (s32[66,1]{1,0:T(8,128)S(1)}, s32[66,1]{1,0:T(8,128)S(1)}, u32[]{:S(2)}, u32[]{:S(2)}) collective-permute-start(s32[66,1]{1,0:T(8,128)S(1)} %get-tuple-element.99), channel_id=1, source_target_pairs={{0,1},{1,2},{2,3},{3,4},{4,5},{5,6},{6,7},{7,8},{8,9},{9,10},{10,1... | collective-permute-start | bytes 800 | tf_op jit(solution)/shard_map/ppermute | solution.py:18
  20.9 7.4 %collective-permute-start.7 = (s32[66,1]{1,0:T(8,128)S(1)}, s32[66,1]{1,0:T(8,128)S(1)}, u32[]{:S(2)}, u32[]{:S(2)}) collective-permute-start(s32[66,1]{1,0:T(8,128)S(1)} %get-tuple-element.100), channel_id=1, source_target_pairs={{1,0},{2,1},{3,2},{4,3},{5,4},{6,5},{7,6},{8,7},{9,8},{10,9},{11,1... | collective-permute-start | bytes 800 | tf_op jit(solution)/shard_map/ppermute | solution.py:21
  29.9 5.9 %collective-permute-start.8 = (f32[1,64]{1,0:T(1,128)S(1)}, f32[1,64]{1,0:T(1,128)S(1)}, u32[]{:S(2)}, u32[]{:S(2)}) collective-permute-start(f32[1,64]{1,0:T(1,128)S(1)} %get-tuple-element.101), channel_id=1, source_target_pairs={{0,32},{32,64},{64,96},{96,128},{128,160},{160,192},{192,224},{224... | collective-permute-start | bytes 776 | tf_op jit(solution)/shard_map/ppermute | solution.py:18
  34.5 5.4 %collective-permute-start.9 = (f32[1,64]{1,0:T(1,128)S(1)}, f32[1,64]{1,0:T(1,128)S(1)}, u32[]{:S(2)}, u32[]{:S(2)}) collective-permute-start(f32[1,64]{1,0:T(1,128)S(1)} %get-tuple-element.102), channel_id=1, source_target_pairs={{32,0},{64,32},{96,64},{128,96},{160,128},{192,160},{224,192},{256... | collective-permute-start | bytes 776 | tf_op jit(solution)/shard_map/ppermute | solution.py:21
  40.0 7.9 %collective-permute-start.10 = (f32[66,1]{1,0:T(8,128)S(1)}, f32[66,1]{1,0:T(8,128)S(1)}, u32[]{:S(2)}, u32[]{:S(2)}) collective-permute-start(f32[66,1]{1,0:T(8,128)S(1)} %get-tuple-element.97), channel_id=1, source_target_pairs={{0,1},{1,2},{2,3},{3,4},{4,5},{5,6},{6,7},{7,8},{8,9},{9,10},{10,1... | collective-permute-start | bytes 800 | tf_op jit(solution)/shard_map/ppermute | solution.py:18
  41.9 7.4 %collective-permute-start.11 = (f32[66,1]{1,0:T(8,128)S(1)}, f32[66,1]{1,0:T(8,128)S(1)}, u32[]{:S(2)}, u32[]{:S(2)}) collective-permute-start(f32[66,1]{1,0:T(8,128)S(1)} %get-tuple-element.98), channel_id=1, source_target_pairs={{1,0},{2,1},{3,2},{4,3},{5,4},{6,5},{7,6},{8,7},{9,8},{10,9},{11,1... | collective-permute-start | bytes 800 | tf_op jit(solution)/shard_map/ppermute | solution.py:21
  49.8 6.3 %copy-start = (f32[64,2112]{1,0:T(8,128)}, f32[64,2112]{1,0:T(8,128)S(1)}, u32[]{:S(2)}) copy-start(f32[64,2112]{1,0:T(8,128)S(1)} %concatenate.75) | copy-start | bytes 1622020
  49.9 16.8 %collective-permute-start.2 = (f32[1,2112]{1,0:T(1,128)S(1)}, f32[1,2112]{1,0:T(1,128)S(1)}, u32[]{:S(2)}, u32[]{:S(2)}) collective-permute-start(f32[1,2112]{1,0:T(1,128)S(1)} %get-tuple-element.79), channel_id=1, source_target_pairs={{0,32},{32,64},{64,96},{96,128},{128,160},{160,192},{192,224},{224... | collective-permute-start | bytes 25352 | tf_op jit(solution)/shard_map/ppermute | solution.py:18
  54.7 11.9 %collective-permute-start.3 = (f32[1,2112]{1,0:T(1,128)S(1)}, f32[1,2112]{1,0:T(1,128)S(1)}, u32[]{:S(2)}, u32[]{:S(2)}) collective-permute-start(f32[1,2112]{1,0:T(1,128)S(1)} %get-tuple-element.80), channel_id=1, source_target_pairs={{32,0},{64,32},{96,64},{128,96},{160,128},{192,160},{224,192},{256... | collective-permute-start | bytes 25352 | tf_op jit(solution)/shard_map/ppermute | solution.py:21
  64.4 2.4 %copy-start.2 = (f32[64,2048]{1,0:T(8,128)S(1)}, f32[64,2048]{1,0:T(8,128)}, u32[]{:S(2)}) copy-start(f32[64,2048]{1,0:T(8,128)} %copy.22) | copy-start | bytes 1572868
  69.0 7.7 %collective-permute-start.12 = (f32[64,32]{1,0:T(8,128)S(1)}, f32[64,32]{1,0:T(8,128)S(1)}, u32[]{:S(2)}, u32[]{:S(2)}) collective-permute-start(f32[64,32]{1,0:T(8,128)S(1)} %get-tuple-element.94), channel_id=1, source_target_pairs={{0,1},{1,2},{2,3},{3,4},{4,5},{5,6},{6,7},{7,8},{8,9},{9,10},{10,1... | collective-permute-start | bytes 24584 | tf_op jit(solution)/shard_map/ppermute | solution.py:18
  71.0 7.3 %collective-permute-start.13 = (f32[64,32]{1,0:T(8,128)S(1)}, f32[64,32]{1,0:T(8,128)S(1)}, u32[]{:S(2)}, u32[]{:S(2)}) collective-permute-start(f32[64,32]{1,0:T(8,128)S(1)} %get-tuple-element.93), channel_id=1, source_target_pairs={{1,0},{2,1},{3,2},{4,3},{5,4},{6,5},{7,6},{8,7},{9,8},{10,9},{11,1... | collective-permute-start | bytes 24584 | tf_op jit(solution)/shard_map/ppermute | solution.py:21
  78.7 7.1 %collective-permute-start.14 = (f32[1,2112]{1,0:T(1,128)S(1)}, f32[1,2112]{1,0:T(1,128)S(1)}, u32[]{:S(2)}, u32[]{:S(2)}) collective-permute-start(f32[1,2112]{1,0:T(1,128)S(1)} %get-tuple-element.77), channel_id=1, source_target_pairs={{0,32},{32,64},{64,96},{96,128},{128,160},{160,192},{192,224},{224... | collective-permute-start | bytes 25352 | tf_op jit(solution)/shard_map/ppermute | solution.py:18
  84.4 6.8 %collective-permute-start.15 = (f32[1,2112]{1,0:T(1,128)S(1)}, f32[1,2112]{1,0:T(1,128)S(1)}, u32[]{:S(2)}, u32[]{:S(2)}) collective-permute-start(f32[1,2112]{1,0:T(1,128)S(1)} %get-tuple-element.78), channel_id=1, source_target_pairs={{32,0},{64,32},{96,64},{128,96},{160,128},{192,160},{224,192},{256... | collective-permute-start | bytes 25352 | tf_op jit(solution)/shard_map/ppermute | solution.py:21
  92.0 7.7 %collective-permute-start.16 = (f32[64,32]{1,0:T(8,128)S(1)}, f32[64,32]{1,0:T(8,128)S(1)}, u32[]{:S(2)}, u32[]{:S(2)}) collective-permute-start(f32[64,32]{1,0:T(8,128)S(1)} %get-tuple-element.92), channel_id=1, source_target_pairs={{0,1},{1,2},{2,3},{3,4},{4,5},{5,6},{6,7},{7,8},{8,9},{9,10},{10,1... | collective-permute-start | bytes 24584 | tf_op jit(solution)/shard_map/ppermute | solution.py:18
  94.0 7.3 %collective-permute-start.17 = (f32[64,32]{1,0:T(8,128)S(1)}, f32[64,32]{1,0:T(8,128)S(1)}, u32[]{:S(2)}, u32[]{:S(2)}) collective-permute-start(f32[64,32]{1,0:T(8,128)S(1)} %get-tuple-element.91), channel_id=1, source_target_pairs={{1,0},{2,1},{3,2},{4,3},{5,4},{6,5},{7,6},{8,7},{9,8},{10,9},{11,1... | collective-permute-start | bytes 24584 | tf_op jit(solution)/shard_map/ppermute | solution.py:21
  101.7 5.3 %collective-permute-start.18 = (f32[1,2112]{1,0:T(1,128)S(1)}, f32[1,2112]{1,0:T(1,128)S(1)}, u32[]{:S(2)}, u32[]{:S(2)}) collective-permute-start(f32[1,2112]{1,0:T(1,128)S(1)} %get-tuple-element.75), channel_id=1, source_target_pairs={{0,32},{32,64},{64,96},{96,128},{128,160},{160,192},{192,224},{224... | collective-permute-start | bytes 25352 | tf_op jit(solution)/shard_map/ppermute | solution.py:18
  105.6 5.6 %collective-permute-start.19 = (f32[1,2112]{1,0:T(1,128)S(1)}, f32[1,2112]{1,0:T(1,128)S(1)}, u32[]{:S(2)}, u32[]{:S(2)}) collective-permute-start(f32[1,2112]{1,0:T(1,128)S(1)} %get-tuple-element.76), channel_id=1, source_target_pairs={{32,0},{64,32},{96,64},{128,96},{160,128},{192,160},{224,192},{256... | collective-permute-start | bytes 25352 | tf_op jit(solution)/shard_map/ppermute | solution.py:21
  112.0 7.7 %collective-permute-start.20 = (f32[64,32]{1,0:T(8,128)S(1)}, f32[64,32]{1,0:T(8,128)S(1)}, u32[]{:S(2)}, u32[]{:S(2)}) collective-permute-start(f32[64,32]{1,0:T(8,128)S(1)} %get-tuple-element.90), channel_id=1, source_target_pairs={{0,1},{1,2},{2,3},{3,4},{4,5},{5,6},{6,7},{7,8},{8,9},{9,10},{10,1... | collective-permute-start | bytes 24584 | tf_op jit(solution)/shard_map/ppermute | solution.py:18
  113.9 7.3 %collective-permute-start.21 = (f32[64,32]{1,0:T(8,128)S(1)}, f32[64,32]{1,0:T(8,128)S(1)}, u32[]{:S(2)}, u32[]{:S(2)}) collective-permute-start(f32[64,32]{1,0:T(8,128)S(1)} %get-tuple-element.89), channel_id=1, source_target_pairs={{1,0},{2,1},{3,2},{4,3},{5,4},{6,5},{7,6},{8,7},{9,8},{10,9},{11,1... | collective-permute-start | bytes 24584 | tf_op jit(solution)/shard_map/ppermute | solution.py:21
  121.6 5.7 %collective-permute-start.22 = (f32[1,2112]{1,0:T(1,128)S(1)}, f32[1,2112]{1,0:T(1,128)S(1)}, u32[]{:S(2)}, u32[]{:S(2)}) collective-permute-start(f32[1,2112]{1,0:T(1,128)S(1)} %get-tuple-element.73), channel_id=1, source_target_pairs={{0,32},{32,64},{64,96},{96,128},{128,160},{160,192},{192,224},{224... | collective-permute-start | bytes 25352 | tf_op jit(solution)/shard_map/ppermute | solution.py:18
  126.0 6.0 %collective-permute-start.23 = (f32[1,2112]{1,0:T(1,128)S(1)}, f32[1,2112]{1,0:T(1,128)S(1)}, u32[]{:S(2)}, u32[]{:S(2)}) collective-permute-start(f32[1,2112]{1,0:T(1,128)S(1)} %get-tuple-element.74), channel_id=1, source_target_pairs={{32,0},{64,32},{96,64},{128,96},{160,128},{192,160},{224,192},{256... | collective-permute-start | bytes 25352 | tf_op jit(solution)/shard_map/ppermute | solution.py:21
  132.8 7.7 %collective-permute-start.24 = (f32[64,32]{1,0:T(8,128)S(1)}, f32[64,32]{1,0:T(8,128)S(1)}, u32[]{:S(2)}, u32[]{:S(2)}) collective-permute-start(f32[64,32]{1,0:T(8,128)S(1)} %get-tuple-element.88), channel_id=1, source_target_pairs={{0,1},{1,2},{2,3},{3,4},{4,5},{5,6},{6,7},{7,8},{8,9},{9,10},{10,1... | collective-permute-start | bytes 24584 | tf_op jit(solution)/shard_map/ppermute | solution.py:18
  134.7 7.3 %collective-permute-start.25 = (f32[64,32]{1,0:T(8,128)S(1)}, f32[64,32]{1,0:T(8,128)S(1)}, u32[]{:S(2)}, u32[]{:S(2)}) collective-permute-start(f32[64,32]{1,0:T(8,128)S(1)} %get-tuple-element.87), channel_id=1, source_target_pairs={{1,0},{2,1},{3,2},{4,3},{5,4},{6,5},{7,6},{8,7},{9,8},{10,9},{11,1... | collective-permute-start | bytes 24584 | tf_op jit(solution)/shard_map/ppermute | solution.py:21
  142.4 6.5 %collective-permute-start.26 = (f32[1,2112]{1,0:T(1,128)S(1)}, f32[1,2112]{1,0:T(1,128)S(1)}, u32[]{:S(2)}, u32[]{:S(2)}) collective-permute-start(f32[1,2112]{1,0:T(1,128)S(1)} %get-tuple-element.71), channel_id=1, source_target_pairs={{0,32},{32,64},{64,96},{96,128},{128,160},{160,192},{192,224},{224... | collective-permute-start | bytes 25352 | tf_op jit(solution)/shard_map/ppermute | solution.py:18
  147.5 5.6 %collective-permute-start.27 = (f32[1,2112]{1,0:T(1,128)S(1)}, f32[1,2112]{1,0:T(1,128)S(1)}, u32[]{:S(2)}, u32[]{:S(2)}) collective-permute-start(f32[1,2112]{1,0:T(1,128)S(1)} %get-tuple-element.72), channel_id=1, source_target_pairs={{32,0},{64,32},{96,64},{128,96},{160,128},{192,160},{224,192},{256... | collective-permute-start | bytes 25352 | tf_op jit(solution)/shard_map/ppermute | solution.py:21
  153.9 7.7 %collective-permute-start.28 = (f32[64,32]{1,0:T(8,128)S(1)}, f32[64,32]{1,0:T(8,128)S(1)}, u32[]{:S(2)}, u32[]{:S(2)}) collective-permute-start(f32[64,32]{1,0:T(8,128)S(1)} %get-tuple-element.86), channel_id=1, source_target_pairs={{0,1},{1,2},{2,3},{3,4},{4,5},{5,6},{6,7},{7,8},{8,9},{9,10},{10,1... | collective-permute-start | bytes 24584 | tf_op jit(solution)/shard_map/ppermute | solution.py:18
  155.9 7.3 %collective-permute-start.29 = (f32[64,32]{1,0:T(8,128)S(1)}, f32[64,32]{1,0:T(8,128)S(1)}, u32[]{:S(2)}, u32[]{:S(2)}) collective-permute-start(f32[64,32]{1,0:T(8,128)S(1)} %get-tuple-element.85), channel_id=1, source_target_pairs={{1,0},{2,1},{3,2},{4,3},{5,4},{6,5},{7,6},{8,7},{9,8},{10,9},{11,1... | collective-permute-start | bytes 24584 | tf_op jit(solution)/shard_map/ppermute | solution.py:21
  163.5 5.4 %collective-permute-start.30 = (f32[1,2112]{1,0:T(1,128)S(1)}, f32[1,2112]{1,0:T(1,128)S(1)}, u32[]{:S(2)}, u32[]{:S(2)}) collective-permute-start(f32[1,2112]{1,0:T(1,128)S(1)} %get-tuple-element.69), channel_id=1, source_target_pairs={{0,32},{32,64},{64,96},{96,128},{128,160},{160,192},{192,224},{224... | collective-permute-start | bytes 25352 | tf_op jit(solution)/shard_map/ppermute | solution.py:18
  167.5 5.6 %collective-permute-start.31 = (f32[1,2112]{1,0:T(1,128)S(1)}, f32[1,2112]{1,0:T(1,128)S(1)}, u32[]{:S(2)}, u32[]{:S(2)}) collective-permute-start(f32[1,2112]{1,0:T(1,128)S(1)} %get-tuple-element.70), channel_id=1, source_target_pairs={{32,0},{64,32},{96,64},{128,96},{160,128},{192,160},{224,192},{256... | collective-permute-start | bytes 25352 | tf_op jit(solution)/shard_map/ppermute | solution.py:21
  173.9 7.7 %collective-permute-start.32 = (f32[64,32]{1,0:T(8,128)S(1)}, f32[64,32]{1,0:T(8,128)S(1)}, u32[]{:S(2)}, u32[]{:S(2)}) collective-permute-start(f32[64,32]{1,0:T(8,128)S(1)} %get-tuple-element.84), channel_id=1, source_target_pairs={{0,1},{1,2},{2,3},{3,4},{4,5},{5,6},{6,7},{7,8},{8,9},{9,10},{10,1... | collective-permute-start | bytes 24584 | tf_op jit(solution)/shard_map/ppermute | solution.py:18
  175.8 7.3 %collective-permute-start.33 = (f32[64,32]{1,0:T(8,128)S(1)}, f32[64,32]{1,0:T(8,128)S(1)}, u32[]{:S(2)}, u32[]{:S(2)}) collective-permute-start(f32[64,32]{1,0:T(8,128)S(1)} %get-tuple-element.83), channel_id=1, source_target_pairs={{1,0},{2,1},{3,2},{4,3},{5,4},{6,5},{7,6},{8,7},{9,8},{10,9},{11,1... | collective-permute-start | bytes 24584 | tf_op jit(solution)/shard_map/ppermute | solution.py:21
  183.5 5.7 %collective-permute-start.34 = (f32[1,2112]{1,0:T(1,128)S(1)}, f32[1,2112]{1,0:T(1,128)S(1)}, u32[]{:S(2)}, u32[]{:S(2)}) collective-permute-start(f32[1,2112]{1,0:T(1,128)S(1)} %get-tuple-element.67), channel_id=1, source_target_pairs={{0,32},{32,64},{64,96},{96,128},{128,160},{160,192},{192,224},{224... | collective-permute-start | bytes 25352 | tf_op jit(solution)/shard_map/ppermute | solution.py:18
  187.8 5.6 %collective-permute-start.35 = (f32[1,2112]{1,0:T(1,128)S(1)}, f32[1,2112]{1,0:T(1,128)S(1)}, u32[]{:S(2)}, u32[]{:S(2)}) collective-permute-start(f32[1,2112]{1,0:T(1,128)S(1)} %get-tuple-element.68), channel_id=1, source_target_pairs={{32,0},{64,32},{96,64},{128,96},{160,128},{192,160},{224,192},{256... | collective-permute-start | bytes 25352 | tf_op jit(solution)/shard_map/ppermute | solution.py:21
  194.3 7.7 %collective-permute-start.36 = (f32[64,32]{1,0:T(8,128)S(1)}, f32[64,32]{1,0:T(8,128)S(1)}, u32[]{:S(2)}, u32[]{:S(2)}) collective-permute-start(f32[64,32]{1,0:T(8,128)S(1)} %get-tuple-element.82), channel_id=1, source_target_pairs={{0,1},{1,2},{2,3},{3,4},{4,5},{5,6},{6,7},{7,8},{8,9},{9,10},{10,1... | collective-permute-start | bytes 24584 | tf_op jit(solution)/shard_map/ppermute | solution.py:18
  196.2 7.3 %collective-permute-start.37 = (f32[64,32]{1,0:T(8,128)S(1)}, f32[64,32]{1,0:T(8,128)S(1)}, u32[]{:S(2)}, u32[]{:S(2)}) collective-permute-start(f32[64,32]{1,0:T(8,128)S(1)} %get-tuple-element.81), channel_id=1, source_target_pairs={{1,0},{2,1},{3,2},{4,3},{5,4},{6,5},{7,6},{8,7},{9,8},{10,9},{11,1... | collective-permute-start | bytes 24584 | tf_op jit(solution)/shard_map/ppermute | solution.py:21
  203.9 5.3 %collective-permute-start.38 = (f32[1,2112]{1,0:T(1,128)S(1)}, f32[1,2112]{1,0:T(1,128)S(1)}, u32[]{:S(2)}, u32[]{:S(2)}) collective-permute-start(f32[1,2112]{1,0:T(1,128)S(1)} %get-tuple-element.65), channel_id=1, source_target_pairs={{0,32},{32,64},{64,96},{96,128},{128,160},{160,192},{192,224},{224... | collective-permute-start | bytes 25352 | tf_op jit(solution)/shard_map/ppermute | solution.py:18
  207.8 5.6 %collective-permute-start.39 = (f32[1,2112]{1,0:T(1,128)S(1)}, f32[1,2112]{1,0:T(1,128)S(1)}, u32[]{:S(2)}, u32[]{:S(2)}) collective-permute-start(f32[1,2112]{1,0:T(1,128)S(1)} %get-tuple-element.66), channel_id=1, source_target_pairs={{32,0},{64,32},{96,64},{128,96},{160,128},{192,160},{224,192},{256... | collective-permute-start | bytes 25352 | tf_op jit(solution)/shard_map/ppermute | solution.py:21
  217.7 5.6 %collective-permute-start.40 = (f32[32,32]{1,0:T(8,128)S(1)}, f32[32,32]{1,0:T(8,128)S(1)}, u32[]{:S(2)}, u32[]{:S(2)}) collective-permute-start(f32[32,32]{1,0:T(8,128)S(1)} %gather_fusion), channel_id=1, source_target_pairs={{0,32},{32,0},{64,96},{96,64},{128,160},{160,128},{192,224},{224,1... | collective-permute-start | bytes 12296 | tf_op jit(solution)/shard_map/ppermute | solution.py:33
  223.8 3.1 %collective-permute-start.41 = (f32[32,32]{1,0:T(8,128)S(1)}, f32[32,32]{1,0:T(8,128)S(1)}, u32[]{:S(2)}, u32[]{:S(2)}) collective-permute-start(f32[32,32]{1,0:T(8,128)S(1)} %min.216), channel_id=1, source_target_pairs={{0,1},{1,0},{2,3},{3,2},{4,5},{5,4},{6,7},{7,6},{8,9},{9,8},{10,11... | collective-permute-start | bytes 12296 | tf_op jit(solution)/shard_map/ppermute | solution.py:33
  227.3 6.5 %collective-permute-start.42 = (f32[32,32]{1,0:T(8,128)S(1)}, f32[32,32]{1,0:T(8,128)S(1)}, u32[]{:S(2)}, u32[]{:S(2)}) collective-permute-start(f32[32,32]{1,0:T(8,128)S(1)} %min.217), channel_id=1, source_target_pairs={{0,64},{64,0},{32,96},{96,32},{128,192},{192,128},{160,224},{224,1... | collective-permute-start | bytes 12296 | tf_op jit(solution)/shard_map/ppermute | solution.py:33
  234.3 5.6 %collective-permute-start.43 = (f32[32,32]{1,0:T(8,128)S(1)}, f32[32,32]{1,0:T(8,128)S(1)}, u32[]{:S(2)}, u32[]{:S(2)}) collective-permute-start(f32[32,32]{1,0:T(8,128)S(1)} %min.218), channel_id=1, source_target_pairs={{0,2},{2,0},{1,3},{3,1},{4,6},{6,4},{5,7},{7,5},{8,10},{10,8},{9,1... | collective-permute-start | bytes 12296 | tf_op jit(solution)/shard_map/ppermute | solution.py:33
  (1 other events, 2.3 us)
where the time goes:
time: 243 us; the launch traced here: 241 us
  starting transfers between devices  147 us (60%)
  waiting for transfers between devices  57.2 us (24%)
  local copies, waits for them, and re-layouts  20.6 us (8%)
  other arithmetic  15 us (6%)
    ppermute x20, starting transfers between devices, with_halo(): lax.ppermute(lax.slice_in_dim(block, 0, width, axis=dim), axis, backward)  70.6 us
    ppermute x20, starting transfers between devices, with_halo(): lax.ppermute(lax.slice_in_dim(block, block.shape[dim] - width, None, axis...  63.7 us
    ppermute x20, waiting for transfers between devices, with_halo(): lax.ppermute(lax.slice_in_dim(block, 0, width, axis=dim), axis, backward)  48.3 us
    ppermute x4, starting transfers between devices, swapped(): return lax.ppermute(block, axis, route)  12.3 us
    ppermute x4, waiting for transfers between devices, swapped(): return lax.ppermute(block, axis, route)  8.5 us
    unnamed x15, local copies, waits for them, and re-layouts  8.1 us
    min x7, other arithmetic, relax_flat(): return jnp.minimum(centre_cells, nearest)  5.92 us
  transfers between devices with their start and end apart: 44, of which 27 were waited for; matrix products, arithmetic and copies ran while one was open for 7% of the time, Pallas kernels for 0%

commit v1 on v0

v1 whole, which is shorter than its diff:
```python
import functools

import jax
import jax.numpy as jnp
from jax import lax
from jax.experimental import pallas as pl
from jax.experimental.pallas import tpu as pltpu
from jax.sharding import PartitionSpec as P

TILE = 64
PORTALS = 32
SWEEPS = 8
HALO = 8
EXT = TILE + 2 * HALO
LANES = 128
CELLS = LANES // PORTALS
GROUPS = EXT // CELLS
SIDE = HALO // CELLS
STEP = EXT // 8
STRIP = 16
FAR = 1000000.0

AROUND = ((-1, 0), (1, 0), (0, -1), (0, 1), (-1, -1), (-1, 1), (1, -1), (1, 1))


def lane_take(values, index):
    return jnp.take_along_axis(values, index, axis=1, mode="promise_in_bounds")


def kernel(
    portal_smem, heights_hbm, blocked_hbm, estimate_hbm, portal_hbm,
    relaxed_hbm, merged_hbm,
    heights, blocked, estimate, portal, relaxed, merged,
    ground, strips, ground_in, high, cost_rows,
    field, cost, dist, rows, shifts, table, table_in, right_rows,
    load_sem, store_sem, ground_send, ground_recv, field_send, field_recv,
    table_send, table_recv,
):
    row_index, col_index = lax.axis_index("row"), lax.axis_index("col")
    row_count, col_count = lax.axis_size("row"), lax.axis_size("col")
    around = [
        (lax.rem(row_index + dr + row_count, row_count), lax.rem(col_index + dc + col_count, col_count))
        for dr, dc in AROUND
    ]

    def other(index, bit):
        return index + bit - 2 * bit * lax.rem(index // bit, 2)

    partners = []
    for level in range(2):
        bit = 1 << level
        partners.append(
            [
                (other(row_index, bit), col_index),
                (row_index, other(col_index, bit)),
                (other(row_index, bit), other(col_index, bit)),
            ]
        )

    loads = [
        pltpu.make_async_copy(source, target, load_sem.at[at])
        for at, (source, target) in enumerate(
            (
                (heights_hbm, heights),
                (blocked_hbm, blocked),
                (portal_hbm, portal),
                (estimate_hbm, estimate),
            )
        )
    ]
    for load in loads:
        load.start()

    barrier = pltpu.get_barrier_semaphore()
    met = around + partners[1]
    for device in met:
        pl.semaphore_signal(barrier, inc=1, device_id=device, device_id_type=pl.DeviceIdType.MESH)

    def send(source, target, send_sem, recv_sem, device):
        copy = pltpu.make_async_remote_copy(
            src_ref=source, dst_ref=target, send_sem=send_sem, recv_sem=recv_sem,
            device_id=device, device_id_type=pl.DeviceIdType.MESH,
        )
        copy.start()
        return copy

    lane = lax.broadcasted_iota(jnp.int32, (8, LANES), 1)
    sublane = lax.broadcasted_iota(jnp.int32, (8, LANES), 0)
    lane_block = lane // PORTALS
    lane_class = lane % PORTALS

    loads[0].wait()
    loads[1].wait()
    ground[:, 0:TILE] = heights[...]
    ground[:, TILE : 2 * TILE] = blocked[...]
    wide = lax.broadcasted_iota(jnp.int32, (STRIP, LANES), 1)
    west = jnp.zeros((STRIP, LANES), jnp.int32)
    east = jnp.zeros((STRIP, LANES), jnp.int32)
    for part in range(4):
        here = ground[part * STRIP : (part + 1) * STRIP]
        base = part * 32
        in_height = (wide >= base) & (wide < base + 16)
        in_block = (wide >= base + 16) & (wide < base + 32)
        west = jnp.where(in_height, pltpu.roll(here, base % LANES, 1), west)
        west = jnp.where(in_block, pltpu.roll(here, (base + 16 - 64) % LANES, 1), west)
        east = jnp.where(in_height, pltpu.roll(here, (base - 48) % LANES, 1), east)
        east = jnp.where(in_block, pltpu.roll(here, (base + 16 - 112) % LANES, 1), east)
    strips[0] = west
    strips[1] = east

    pl.semaphore_wait(barrier, len(met))

    top, bottom = ground.at[0:STRIP], ground.at[TILE - STRIP : TILE]
    ground_source = {-1: top, 1: bottom}
    ground_copies = []
    for at, (dr, dc) in enumerate(AROUND):
        if dr:
            source = ground_source[dr]
        else:
            source = strips.at[0 if dc < 0 else 1]
        slot = AROUND.index((-dr, -dc))
        ground_copies.append(
            send(source, ground_in.at[slot], ground_send.at[at], ground_recv.at[slot], around[at])
        )

    loads[2].wait()
    own = jnp.broadcast_to(portal[0, 0:1, :], (8, PORTALS))
    portal_cells = jnp.concatenate([own] * CELLS, axis=1)
    loads[3].wait()

    def prepare(part, group):
        values = estimate[part * 16 : (part + 1) * 16, group * LANES : (group + 1) * LANES]
        values = values.astype(jnp.float32)
        for half in range(2):
            row = part * 16 + half * 8
            cell = (row + sublane) * TILE + lane_block + group * CELLS
            here = jnp.where(portal_cells == cell, 0.0, values[half * 8 : (half + 1) * 8])
            field[SIDE + group, HALO + row : HALO + row + 8, :] = here

    inner = TILE // CELLS
    for part in (0, 3):
        for group in range(inner):
            prepare(part, group)
    for part in (1, 2):
        for group in (0, 1, inner - 2, inner - 1):
            prepare(part, group)

    def span(step, own_start, length, halo):
        if step < 0:
            return (own_start, halo), (own_start + length, halo)
        if step > 0:
            return (own_start + length - halo, halo), (own_start - halo, halo)
        return (own_start, length), (own_start, length)

    field_copies = []
    for at, (dr, dc) in enumerate(AROUND):
        (row_from, row_len), (row_to, _) = span(dr, HALO, TILE, HALO)
        (grp_from, grp_len), (grp_to, _) = span(dc, SIDE, inner, SIDE)
        slot = AROUND.index((-dr, -dc))
        field_copies.append(
            send(
                field.at[pl.ds(grp_from, grp_len), pl.ds(row_from, row_len), :],
                field.at[pl.ds(grp_to, grp_len), pl.ds(row_to, row_len), :],
                field_send.at[at], field_recv.at[slot], around[at],
            )
        )

    for part in (1, 2):
        for group in range(2, inner - 2):
            prepare(part, group)

    for copy in ground_copies:
        copy.wait_recv()
    slots = {step: at for at, step in enumerate(AROUND)}

    def lay(row, west_height, middle, east_height, west_block, east_block):
        height = jnp.where(wide < 16, west_height, jnp.where(wide < 80, pltpu.roll(middle, 16, 1), east_height))
        block = jnp.where(wide < 16, west_block, jnp.where(wide < 80, pltpu.roll(middle, 80, 1), east_block))
        high[0, row : row + STRIP, :] = height.astype(jnp.float32)
        high[1, row : row + STRIP, :] = block.astype(jnp.float32)

    for dr, row in ((-1, 0), (1, STRIP + TILE)):
        west_in, middle, east_in = (ground_in[slots[(dr, dc)]] for dc in (-1, 0, 1))
        lay(
            row, pltpu.roll(west_in, 80, 1), middle, pltpu.roll(east_in, 80, 1),
            pltpu.roll(west_in, 16, 1), pltpu.roll(east_in, 16, 1),
        )
    west_in, east_in = ground_in[slots[(0, -1)]], ground_in[slots[(0, 1)]]
    for part in range(4):
        base = part * 32
        lay(
            STRIP + part * STRIP,
            pltpu.roll(west_in, (-base) % LANES, 1),
            ground[part * STRIP : (part + 1) * STRIP],
            pltpu.roll(east_in, (80 - base) % LANES, 1),
            pltpu.roll(west_in, (-base - 16) % LANES, 1),
            pltpu.roll(east_in, (64 - base) % LANES, 1),
        )

    @pl.when(row_index == 0)
    def _():
        high[0, STRIP - 1 : STRIP, :] = high[0, STRIP : STRIP + 1, :]

    @pl.when(row_index == row_count - 1)
    def _():
        high[0, STRIP + TILE : STRIP + TILE + 1, :] = high[0, STRIP + TILE - 1 : STRIP + TILE, :]

    shift = STRIP - HALO
    near = high[0, shift : shift + EXT, :]
    up = high[0, shift - 1 : shift - 1 + EXT, :]
    down = high[0, shift + 1 : shift + 1 + EXT, :]
    col = lax.broadcasted_iota(jnp.int32, (EXT, LANES), 1) - STRIP
    row = lax.broadcasted_iota(jnp.int32, (EXT, LANES), 0) - HALO
    grid_col = col_index * TILE + col
    grid_row = row_index * TILE + row
    before = jnp.where(grid_col == 0, near, pltpu.roll(near, 1, 1))
    after = jnp.where(grid_col == col_count * TILE - 1, near, pltpu.roll(near, LANES - 1, 1))
    grad_x = (after - before) * 0.01
    grad_y = (down - up) * 0.01
    grad_sq = grad_x * grad_x + grad_y * grad_y
    step_cost = (
        1.0 + 2.0 * grad_sq + 0.5 * grad_y / jnp.sqrt(1.0 + grad_sq)
        + 30.0 * high[1, shift : shift + EXT, :]
    )
    inside = (
        (grid_row >= 0) & (grid_row < row_count * TILE)
        & (grid_col >= 0) & (grid_col < col_count * TILE)
    )
    cost_rows[...] = jnp.where(inside, step_cost, FAR)
    for at in range(STEP):
        values = cost_rows[pl.ds(at, 8, stride=STEP), :]
        for group in range(GROUPS):
            cost[group, at] = lane_take(values, lane_block + (group * CELLS + shift))

    for copy in field_copies:
        copy.wait_recv()
    for group in range(GROUPS):
        for at in range(STEP):
            here = cost[group, at]
            start = field[group, pl.ds(at, 8, stride=STEP), :] + 0.5 * here
            dist[group, at] = jnp.where(here >= FAR, FAR, start)

    first_block, last_block = lane < PORTALS, lane >= LANES - PORTALS

    def sweep(_, carry):
        now = [dist[0, at] for at in range(STEP)]
        pair_west = now
        for group in range(GROUPS):
            later = [dist[group + 1, at] for at in range(STEP)] if group < GROUPS - 1 else now
            east_of = [
                pltpu.roll(jnp.where(first_block, later[at], now[at]), LANES - PORTALS, 1)
                for at in range(STEP)
            ]
            below = east_of[1:] + [pltpu.roll(east_of[0], 7, 0)]
            pairs = [jnp.minimum(now[at], below[at]) for at in range(STEP)]
            north = [pltpu.roll(pairs[STEP - 1], 1, 0)] + pairs[:-1]
            for at in range(STEP):
                west_of = pltpu.roll(jnp.where(last_block, pair_west[at], pairs[at]), PORTALS, 1)
                nearest = cost[group, at] + jnp.minimum(north[at], west_of)
                dist[group, at] = jnp.minimum(now[at], nearest)
            pair_west, now = pairs, later
        return carry

    lax.fori_loop(0, SWEEPS, sweep, 0)

    for copy in field_copies:
        copy.wait_send()
    for group in range(SIDE, GROUPS - SIDE):
        for at in range(STEP):
            field[group, pl.ds(at, 8, stride=STEP), :] = dist[group, at] - 0.5 * cost[group, at]

    for at in range(PORTALS):
        cell = portal_smem[0, 0, at]
        rows[at : at + 1, :] = field[SIDE + (cell % TILE) // CELLS, pl.ds(HALO + cell // TILE, 1), :]
        shifts[at : at + 1, :] = jnp.full((1, LANES), (cell % CELLS) * PORTALS, jnp.int32)
    first = jnp.zeros((8, LANES), jnp.float32)
    for part in range(4):
        index = shifts[part * 8 : part * 8 + 8, :] + lane_class
        first = jnp.where(lane_block == part, lane_take(rows[part * 8 : part * 8 + 8, :], index), first)
    table[0] = first

    table_copies = []

    def exchange(level):
        copies = [
            send(
                table.at[level], table_in.at[3 * level + at],
                table_send.at[3 * level + at], table_recv.at[3 * level + at], device,
            )
            for at, device in enumerate(partners[level])
        ]
        table_copies.extend(copies)
        return copies

    def left_of(values):
        return [lane_take(values, lane_block * PORTALS + at) for at in range(PORTALS)]

    def right_of(values, slot):
        for part in range(4):
            right_rows[slot, part * 8 : part * 8 + 8, :] = lane_take(values, lane_class + part * PORTALS)
        return [
            jnp.broadcast_to(right_rows[slot, at : at + 1, :], (8, LANES)) for at in range(PORTALS)
        ]

    def minplus(left, right):
        sums = [a + b for a, b in zip(left, right)]
        while len(sums) > 1:
            sums = [jnp.minimum(a, b) for a, b in zip(sums[::2], sums[1::2])]
        return sums[0]

    def pair(near_table, far_table, slot):
        through = minplus(left_of(near_table), right_of(far_table, slot))
        return jnp.minimum(near_table, minplus(left_of(through), right_of(near_table, slot + 1)))

    copies = exchange(0)

    for group in range(inner):
        for part in range(4):
            values = field[SIDE + group, HALO + part * 16 : HALO + part * 16 + 16, :]
            relaxed[part * 16 : part * 16 + 16, group * LANES : (group + 1) * LANES] = values.astype(jnp.bfloat16)
    store = pltpu.make_async_copy(relaxed, relaxed_hbm, store_sem.at[0])
    store.start()

    now = first
    for level in range(2):
        for copy in copies:
            copy.wait_recv()
        by_row, by_col, by_both = (table_in[3 * level + at] for at in range(3))
        here = pair(now, by_row, 6 * level)
        there = pair(by_col, by_both, 6 * level + 2)
        now = pair(here, there, 6 * level + 4)
        if level == 0:
            table[1] = now
            copies = exchange(1)
    now = now * 0.0625
    for part in range(4):
        merged[0, 0, part * 8 : part * 8 + 8, :] = now[:, part * PORTALS : (part + 1) * PORTALS]
    last = pltpu.make_async_copy(merged, merged_hbm, store_sem.at[1])
    last.start()

    for copy in ground_copies + table_copies:
        copy.wait_send()
    store.wait()
    last.wait()


def body(heights, blocked, estimate, portal_index):
    anywhere = pl.BlockSpec(memory_space=pl.ANY)
    return pl.pallas_call(
        kernel,
        out_shape=(
            jax.ShapeDtypeStruct(estimate.shape, jnp.bfloat16),
            jax.ShapeDtypeStruct((1, 1, PORTALS, PORTALS), jnp.float32),
        ),
        in_specs=[pl.BlockSpec(memory_space=pltpu.SMEM)] + [anywhere] * 4,
        out_specs=(anywhere, anywhere),
        scratch_shapes=[
            pltpu.VMEM((TILE, TILE), jnp.int32),
            pltpu.VMEM((TILE, TILE), jnp.int32),
            pltpu.VMEM((TILE, TILE * PORTALS), jnp.bfloat16),
            pltpu.VMEM((1, 1, PORTALS), jnp.int32),
            pltpu.VMEM((TILE, TILE * PORTALS), jnp.bfloat16),
            pltpu.VMEM((1, 1, PORTALS, PORTALS), jnp.float32),
            pltpu.VMEM((TILE, LANES), jnp.int32),
            pltpu.VMEM((2, STRIP, LANES), jnp.int32),
            pltpu.VMEM((8, STRIP, LANES), jnp.int32),
            pltpu.VMEM((2, TILE + 2 * STRIP, LANES), jnp.float32),
            pltpu.VMEM((EXT, LANES), jnp.float32),
            pltpu.VMEM((GROUPS, EXT, LANES), jnp.float32),
            pltpu.VMEM((GROUPS, STEP, 8, LANES), jnp.float32),
            pltpu.VMEM((GROUPS, STEP, 8, LANES), jnp.float32),
            pltpu.VMEM((PORTALS, LANES), jnp.float32),
            pltpu.VMEM((PORTALS, LANES), jnp.int32),
            pltpu.VMEM((2, 8, LANES), jnp.float32),
            pltpu.VMEM((6, 8, LANES), jnp.float32),
            pltpu.VMEM((12, PORTALS, LANES), jnp.float32),
            pltpu.SemaphoreType.DMA((4,)),
            pltpu.SemaphoreType.DMA((2,)),
            pltpu.SemaphoreType.DMA((8,)),
            pltpu.SemaphoreType.DMA((8,)),
            pltpu.SemaphoreType.DMA((8,)),
            pltpu.SemaphoreType.DMA((8,)),
            pltpu.SemaphoreType.DMA((6,)),
            pltpu.SemaphoreType.DMA((6,)),
        ],
        compiler_params=pltpu.CompilerParams(
            collective_id=0, has_side_effects=True, vmem_limit_bytes=16 * 2**20
        ),
    )(portal_index, heights, blocked, estimate, portal_index)


def solution(mesh):
    placed = (P("row", "col"), P("row", "col"), P("row", "col"), P("row", "col", None))
    return jax.shard_map(
        body,
        mesh=mesh,
        in_specs=placed,
        out_specs=(P("row", "col"), P("row", "col", None, None)),
        check_vma=False,
    )
```

time: 243 us -> 43.1 us (0.18)
  the two profiles are of different devices: /device:TPU:4 before, /device:TPU:8 now
where the time goes in v1:
time: 43.1 us; the launch traced here: 42.8 us
  Pallas kernels  37.7 us (87%)
  local copies, waits for them, and re-layouts  4.42 us (10%)
  between operations  0.65 us (2%)
    pallas_call x1, Pallas kernels, body(): pl.pallas_call(kernel, out_shape=(jax.ShapeDtypeStruct(estimate.shape, jn...  37.7 us
    unnamed x10, local copies, waits for them, and re-layouts  4.42 us

profile of v1, /device:TPU:8, one launch (start us, length us, event | category | flops | bytes accessed | tf_op | source)
XLA Modules:
  0.0 42.8 jit_solution(11461393348731484978)
XLA Ops:
  0.6 0.0 copy-start
  0.6 0.9 %copy-done = bf16[64,2048]{1,0:T(8,128)(2,1)S(1)} copy-done((bf16[64,2048]{1,0:T(8,128)(2,1)S(1)}, bf16[64,2048]{1,0:T(8,128)(2,1)}, u32[]{:S(2)}) %copy-start) | copy-done | bytes 262168
  1.6 0.0 copy-start.1
  1.6 0.8 %copy-done.1 = s32[64,64]{1,0:T(8,128)S(1)} copy-done((s32[64,64]{1,0:T(8,128)S(1)}, s32[64,64]{1,0:T(8,128)}, u32[]{:S(2)}) %copy-start.1) | copy-done | bytes 16408
  2.3 0.0 copy-start.2
  2.3 0.8 %copy-done.2 = s32[64,64]{1,0:T(8,128)S(1)} copy-done((s32[64,64]{1,0:T(8,128)S(1)}, s32[64,64]{1,0:T(8,128)}, u32[]{:S(2)}) %copy-start.2) | copy-done | bytes 16408
  3.1 0.0 copy-start.3
  3.1 0.7 %copy-done.3 = s32[1,1,32]{2,1,0:T(1,128)S(1)} copy-done((s32[1,1,32]{2,1,0:T(1,128)S(1)}, s32[1,1,32]{2,1,0:T(1,128)}, u32[]{:S(2)}) %copy-start.3) | copy-done | bytes 152
  3.8 37.7 %shard_map.59 = (bf16[64,2048]{1,0:T(8,128)(2,1)S(1)}, f32[1,1,32,32]{3,2,1,0:T(8,128)S(1)}) custom-call(s32[1,1,32]{2,1,0:T(1,128)S(1)} %copy-done.3, s32[64,64]{1,0:T(8,128)S(1)} %copy-done.1, s32[64,64]{1,0:T(8,128)S(1)} %copy-done.2, bf16[64,2048]{1,0:T(8,128)(2,1)S(1)} %copy-done, s32[1,1,32]{2,1,0:T(1,128)S(1)} %copy-done.3), custom_call_target="tpu_custom_call" | custom-call | tf_op jit(solution)/shard_map/pallas_call | solution.py:349
  41.5 0.7 %copy.8 = bf16[64,2048]{1,0:T(8,128)(2,1)} copy(bf16[64,2048]{1,0:T(8,128)(2,1)S(1)} %get-tuple-element.4) | data formatting | bytes 524288
  42.2 0.6 %copy.9 = f32[1,1,32,32]{3,2,1,0:T(8,128)} copy(f32[1,1,32,32]{3,2,1,0:T(8,128)S(1)} %get-tuple-element.5) | data formatting | bytes 8192
Async XLA Ops:
  0.6 1.0 %copy-start = (bf16[64,2048]{1,0:T(8,128)(2,1)S(1)}, bf16[64,2048]{1,0:T(8,128)(2,1)}, u32[]{:S(2)}) copy-start(bf16[64,2048]{1,0:T(8,128)(2,1)} %estimate_hbm.1) | copy-start | bytes 786436
  1.6 0.8 %copy-start.1 = (s32[64,64]{1,0:T(8,128)S(1)}, s32[64,64]{1,0:T(8,128)}, u32[]{:S(2)}) copy-start(s32[64,64]{1,0:T(8,128)} %heights_hbm.1) | copy-start | bytes 49156
  2.3 0.8 %copy-start.2 = (s32[64,64]{1,0:T(8,128)S(1)}, s32[64,64]{1,0:T(8,128)}, u32[]{:S(2)}) copy-start(s32[64,64]{1,0:T(8,128)} %blocked_hbm.1) | copy-start | bytes 49156
  3.1 0.7 %copy-start.3 = (s32[1,1,32]{2,1,0:T(1,128)S(1)}, s32[1,1,32]{2,1,0:T(1,128)}, u32[]{:S(2)}) copy-start(s32[1,1,32]{2,1,0:T(1,128)} %portal_hbm.1) | copy-start | bytes 388

commit v2 on v1

--- a/solution.py
+++ b/solution.py
@@ -13,13 +13,14 @@
 HALO = 8
 EXT = TILE + 2 * HALO
 LANES = 128
-CELLS = LANES // PORTALS
-GROUPS = EXT // CELLS
-SIDE = HALO // CELLS
+BLOCKS = LANES // PORTALS
+OWN = TILE // BLOCKS
+GROUPS = EXT // BLOCKS
 STEP = EXT // 8
 STRIP = 16
 FAR = 1000000.0
 
+
 AROUND = ((-1, 0), (1, 0), (0, -1), (0, 1), (-1, -1), (-1, 1), (1, -1), (1, 1))
 
 
@@ -28,13 +29,12 @@
 
 
 def kernel(
-    portal_smem, heights_hbm, blocked_hbm, estimate_hbm, portal_hbm,
-    relaxed_hbm, merged_hbm,
-    heights, blocked, estimate, portal, relaxed, merged,
+    heights_hbm, blocked_hbm, estimate_hbm, portal_hbm,
+    relaxed, merged,
+    heights, blocked, estimate, portal, portal_smem,
     ground, strips, ground_in, high, cost_rows,
-    field, cost, dist, rows, shifts, table, table_in, right_rows,
-    load_sem, store_sem, ground_send, ground_recv, field_send, field_recv,
-    table_send, table_recv,
+    field, side_out, side_in, cost, dist, rows, shifts, table, table_in, right_rows,
+    load_sem, ground_send, ground_recv, field_send, field_recv, table_send, table_recv,
 ):
     row_index, col_index = lax.axis_index("row"), lax.axis_index("col")
     row_count, col_count = lax.axis_size("row"), lax.axis_size("col")
@@ -64,7 +64,10 @@
                 (heights_hbm, heights),
                 (blocked_hbm, blocked),
                 (portal_hbm, portal),
-                (estimate_hbm, estimate),
+                (estimate_hbm.at[0:16], estimate.at[0:16]),
+                (estimate_hbm.at[48:64], estimate.at[48:64]),
+                (estimate_hbm.at[16:48], estimate.at[16:48]),
+                (portal_hbm, portal_smem),
             )
         )
     ]
@@ -125,49 +128,79 @@
 
     loads[2].wait()
     own = jnp.broadcast_to(portal[0, 0:1, :], (8, PORTALS))
-    portal_cells = jnp.concatenate([own] * CELLS, axis=1)
+    portal_cells = jnp.concatenate([own] * BLOCKS, axis=1)
     loads[3].wait()
-
-    def prepare(part, group):
+    loads[4].wait()
+    loads[5].wait()
+    low = lane < 2 * PORTALS
+    even = lane_block % 2 == 0
+    swapped_blocks = lane_class + (lane_block + 1 - 2 * (lane_block % 2)) * PORTALS
+
+    def transposed(a):
+        t = [None] * 4
+        for at in range(2):
+            turned = pltpu.roll(jnp.where(low, a[at + 2], a[at]), 2 * PORTALS, 1)
+            t[at], t[at + 2] = jnp.where(low, a[at], turned), jnp.where(low, turned, a[at + 2])
+        out = [None] * 4
+        for at in (0, 2):
+            turned = lane_take(jnp.where(even, t[at + 1], t[at]), swapped_blocks)
+            out[at], out[at + 1] = jnp.where(even, t[at], turned), jnp.where(even, turned, t[at + 1])
+        return out
+
+    def estimates(part, group):
         values = estimate[part * 16 : (part + 1) * 16, group * LANES : (group + 1) * LANES]
         values = values.astype(jnp.float32)
+        return values[0:8], values[8:16]
+
+    def prepare(part):
+        for first in range(4):
+            halves = [estimates(part, first + 4 * at) for at in range(4)]
+            for half in range(2):
+                row = part * 16 + half * 8
+                cell = (row + sublane) * TILE + lane_block * OWN
+                for at, values in enumerate(transposed([pieces[half] for pieces in halves])):
+                    group = 4 * first + at
+                    field[group, HALO + row : HALO + row + 8, :] = jnp.where(
+                        portal_cells == cell + group, 0.0, values
+                    )
+
+    def edges(part):
+        columns = (0, 1, OWN - 2, OWN - 1)
+        pieces = [estimates(part, group) for group in columns]
         for half in range(2):
             row = part * 16 + half * 8
-            cell = (row + sublane) * TILE + lane_block + group * CELLS
-            here = jnp.where(portal_cells == cell, 0.0, values[half * 8 : (half + 1) * 8])
-            field[SIDE + group, HALO + row : HALO + row + 8, :] = here
-
-    inner = TILE // CELLS
-    for part in (0, 3):
-        for group in range(inner):
-            prepare(part, group)
-    for part in (1, 2):
-        for group in (0, 1, inner - 2, inner - 1):
-            prepare(part, group)
-
-    def span(step, own_start, length, halo):
-        if step < 0:
-            return (own_start, halo), (own_start + length, halo)
-        if step > 0:
-            return (own_start + length - halo, halo), (own_start - halo, halo)
-        return (own_start, length), (own_start, length)
+            cell = (row + sublane) * TILE + lane_block
+            w0, w1, e0, e1 = (
+                jnp.where(portal_cells == cell + group * BLOCKS, 0.0, piece[half])
+                for group, piece in zip(columns, pieces)
+            )
+            side_out[0, 0, row : row + 8, :] = jnp.where(even, w0, pltpu.roll(w1, 32, 1))
+            side_out[0, 1, row : row + 8, :] = jnp.where(even, pltpu.roll(w0, 96, 1), w1)
+            side_out[1, 0, row : row + 8, :] = jnp.where(even, pltpu.roll(e0, 64, 1), pltpu.roll(e1, 96, 1))
+            side_out[1, 1, row : row + 8, :] = jnp.where(even, pltpu.roll(e0, 32, 1), pltpu.roll(e1, 64, 1))
+
+    prepare(0)
+    prepare(3)
+    for part in range(4):
+        edges(part)
 
     field_copies = []
     for at, (dr, dc) in enumerate(AROUND):
-        (row_from, row_len), (row_to, _) = span(dr, HALO, TILE, HALO)
-        (grp_from, grp_len), (grp_to, _) = span(dc, SIDE, inner, SIDE)
+        row_from, row_to, row_len = {
+            -1: (0, HALO + TILE, HALO), 0: (0, HALO, TILE), 1: (TILE - HALO, 0, HALO)
+        }[dr]
+        if dc:
+            side = 0 if dc < 0 else 1
+            source = side_out.at[side, :, pl.ds(row_from, row_len), :]
+            target = side_in.at[side, :, pl.ds(row_to, row_len), :]
+        else:
+            source = field.at[:, pl.ds(HALO + row_from, row_len), :]
+            target = field.at[:, pl.ds(row_to, row_len), :]
         slot = AROUND.index((-dr, -dc))
-        field_copies.append(
-            send(
-                field.at[pl.ds(grp_from, grp_len), pl.ds(row_from, row_len), :],
-                field.at[pl.ds(grp_to, grp_len), pl.ds(row_to, row_len), :],
-                field_send.at[at], field_recv.at[slot], around[at],
-            )
-        )
-
-    for part in (1, 2):
-        for group in range(2, inner - 2):
-            prepare(part, group)
+        field_copies.append(send(source, target, field_send.at[at], field_recv.at[slot], around[at]))
+
+    prepare(1)
+    prepare(2)
 
     for copy in ground_copies:
         copy.wait_recv()
@@ -227,52 +260,79 @@
         & (grid_col >= 0) & (grid_col < col_count * TILE)
     )
     cost_rows[...] = jnp.where(inside, step_cost, FAR)
+    first_column = STRIP + lane_block * OWN
+    halo_shift = jnp.where(low, TILE + 4 * lane_block, 4 * lane_block - 16) - lane_block * OWN
     for at in range(STEP):
         values = cost_rows[pl.ds(at, 8, stride=STEP), :]
         for group in range(GROUPS):
-            cost[group, at] = lane_take(values, lane_block + (group * CELLS + shift))
+            cost[group, at] = lane_take(values, first_column + (group if group < OWN else group - OWN + halo_shift))
 
     for copy in field_copies:
         copy.wait_recv()
-    for group in range(GROUPS):
-        for at in range(STEP):
-            here = cost[group, at]
-            start = field[group, pl.ds(at, 8, stride=STEP), :] + 0.5 * here
-            dist[group, at] = jnp.where(here >= FAR, FAR, start)
-
-    first_block, last_block = lane < PORTALS, lane >= LANES - PORTALS
+
+    def start(group, at, distance):
+        here = cost[group, at]
+        dist[group, at] = jnp.where(here >= FAR, FAR, distance + 0.5 * here)
+
+    for at in range(STEP):
+        for group in range(OWN):
+            start(group, at, field[group, pl.ds(at, 8, stride=STEP), :])
+        for piece in range(2):
+            from_east = side_in[0, piece, pl.ds(at, 8, stride=STEP), :]
+            from_west = side_in[1, piece, pl.ds(at, 8, stride=STEP), :]
+            start(OWN + piece, at, jnp.where(low, from_east, from_west))
+            start(OWN + piece + 2, at, pltpu.roll(jnp.where(low, from_west, from_east), 64, 1))
+
+    first_block, last_block = lane_block == 0, lane_block == BLOCKS - 1
 
     def sweep(_, carry):
-        now = [dist[0, at] for at in range(STEP)]
-        pair_west = now
-        for group in range(GROUPS):
-            later = [dist[group + 1, at] for at in range(STEP)] if group < GROUPS - 1 else now
-            east_of = [
-                pltpu.roll(jnp.where(first_block, later[at], now[at]), LANES - PORTALS, 1)
-                for at in range(STEP)
-            ]
+        def pairs_of(here, east_of):
             below = east_of[1:] + [pltpu.roll(east_of[0], 7, 0)]
-            pairs = [jnp.minimum(now[at], below[at]) for at in range(STEP)]
-            north = [pltpu.roll(pairs[STEP - 1], 1, 0)] + pairs[:-1]
-            for at in range(STEP):
-                west_of = pltpu.roll(jnp.where(last_block, pair_west[at], pairs[at]), PORTALS, 1)
-                nearest = cost[group, at] + jnp.minimum(north[at], west_of)
-                dist[group, at] = jnp.minimum(now[at], nearest)
-            pair_west, now = pairs, later
+            return [jnp.minimum(a, b) for a, b in zip(here, below)]
+
+        def column(group):
+            return [dist[group, at] for at in range(STEP)]
+
+        own_first, halo_first = column(0), column(OWN)
+        own_pairs = pairs_of(
+            column(OWN - 1),
+            [pltpu.roll(jnp.where(first_block, a, b), LANES - PORTALS, 1) for a, b in zip(halo_first, own_first)],
+        )
+        halo_pairs = pairs_of(
+            column(GROUPS - 1),
+            [pltpu.roll(jnp.where(first_block, a, b), LANES - PORTALS, 1) for a, b in zip(own_first, halo_first)],
+        )
+        own_west = [pltpu.roll(jnp.where(last_block, a, b), PORTALS, 1) for a, b in zip(halo_pairs, own_pairs)]
+        halo_west = [pltpu.roll(jnp.where(last_block, a, b), PORTALS, 1) for a, b in zip(own_pairs, halo_pairs)]
+        for begin, end, west_of, end_pairs in ((0, OWN, own_west, own_pairs), (OWN, GROUPS, halo_west, halo_pairs)):
+            now = own_first if begin == 0 else column(begin)
+            for group in range(begin, end):
+                if group < end - 1:
+                    later = column(group + 1)
+                    pairs = pairs_of(now, later)
+                else:
+                    pairs = end_pairs
+                north = [pltpu.roll(pairs[STEP - 1], 1, 0)] + pairs[:-1]
+                for at in range(STEP):
+                    nearest = cost[group, at] + jnp.minimum(north[at], west_of[at])
+                    dist[group, at] = jnp.minimum(now[at], nearest)
+                west_of, now = pairs, later
         return carry
 
     lax.fori_loop(0, SWEEPS, sweep, 0)
 
     for copy in field_copies:
         copy.wait_send()
-    for group in range(SIDE, GROUPS - SIDE):
+    for group in range(OWN):
         for at in range(STEP):
             field[group, pl.ds(at, 8, stride=STEP), :] = dist[group, at] - 0.5 * cost[group, at]
 
+    loads[6].wait()
     for at in range(PORTALS):
         cell = portal_smem[0, 0, at]
-        rows[at : at + 1, :] = field[SIDE + (cell % TILE) // CELLS, pl.ds(HALO + cell // TILE, 1), :]
-        shifts[at : at + 1, :] = jnp.full((1, LANES), (cell % CELLS) * PORTALS, jnp.int32)
+        column_at = cell % TILE
+        rows[at : at + 1, :] = field[column_at % OWN, pl.ds(HALO + cell // TILE, 1), :]
+        shifts[at : at + 1, :] = jnp.full((1, LANES), column_at // OWN * PORTALS, jnp.int32)
     first = jnp.zeros((8, LANES), jnp.float32)
     for part in range(4):
         index = shifts[part * 8 : part * 8 + 8, :] + lane_class
@@ -308,65 +368,73 @@
             sums = [jnp.minimum(a, b) for a, b in zip(sums[::2], sums[1::2])]
         return sums[0]
 
-    def pair(near_table, far_table, slot):
-        through = minplus(left_of(near_table), right_of(far_table, slot))
-        return jnp.minimum(near_table, minplus(left_of(through), right_of(near_table, slot + 1)))
-
-    copies = exchange(0)
-
-    for group in range(inner):
-        for part in range(4):
-            values = field[SIDE + group, HALO + part * 16 : HALO + part * 16 + 16, :]
-            relaxed[part * 16 : part * 16 + 16, group * LANES : (group + 1) * LANES] = values.astype(jnp.bfloat16)
-    store = pltpu.make_async_copy(relaxed, relaxed_hbm, store_sem.at[0])
-    store.start()
+    def pair(near_table, near_left, near_right, far_right):
+        through = minplus(near_left, far_right)
+        return jnp.minimum(near_table, minplus(left_of(through), near_right))
+
+    def relax_out(part):
+        for first_at in range(4):
+            for_rows = [
+                transposed(
+                    [
+                        field[4 * first_at + at, HALO + part * 16 + half * 8 : HALO + part * 16 + half * 8 + 8, :]
+                        for at in range(4)
+                    ]
+                )
+                for half in range(2)
+            ]
+            for at in range(4):
+                group = first_at + 4 * at
+                values = jnp.concatenate([for_rows[0][at], for_rows[1][at]], axis=0)
+                relaxed[part * 16 : part * 16 + 16, group * LANES : (group + 1) * LANES] = values.astype(jnp.bfloat16)
 
     now = first
     for level in range(2):
+        copies = exchange(level)
+        now_left, now_right = left_of(now), right_of(now, 6 * level)
+        relax_out(2 * level)
+        relax_out(2 * level + 1)
         for copy in copies:
             copy.wait_recv()
         by_row, by_col, by_both = (table_in[3 * level + at] for at in range(3))
-        here = pair(now, by_row, 6 * level)
-        there = pair(by_col, by_both, 6 * level + 2)
-        now = pair(here, there, 6 * level + 4)
+        here = pair(now, now_left, now_right, right_of(by_row, 6 * level + 1))
+        there = pair(by_col, left_of(by_col), right_of(by_col, 6 * level + 2), right_of(by_both, 6 * level + 3))
+        now = pair(here, left_of(here), right_of(here, 6 * level + 4), right_of(there, 6 * level + 5))
         if level == 0:
             table[1] = now
-            copies = exchange(1)
     now = now * 0.0625
     for part in range(4):
         merged[0, 0, part * 8 : part * 8 + 8, :] = now[:, part * PORTALS : (part + 1) * PORTALS]
-    last = pltpu.make_async_copy(merged, merged_hbm, store_sem.at[1])
-    last.start()
 
     for copy in ground_copies + table_copies:
         copy.wait_send()
-    store.wait()
-    last.wait()
 
 
 def body(heights, blocked, estimate, portal_index):
-    anywhere = pl.BlockSpec(memory_space=pl.ANY)
+    in_hbm = pl.BlockSpec(memory_space=pltpu.HBM)
+    in_vmem = pl.BlockSpec(memory_space=pltpu.VMEM)
     return pl.pallas_call(
         kernel,
         out_shape=(
             jax.ShapeDtypeStruct(estimate.shape, jnp.bfloat16),
             jax.ShapeDtypeStruct((1, 1, PORTALS, PORTALS), jnp.float32),
         ),
-        in_specs=[pl.BlockSpec(memory_space=pltpu.SMEM)] + [anywhere] * 4,
-        out_specs=(anywhere, anywhere),
+        in_specs=[in_hbm] * 4,
+        out_specs=(in_vmem, in_vmem),
         scratch_shapes=[
             pltpu.VMEM((TILE, TILE), jnp.int32),
             pltpu.VMEM((TILE, TILE), jnp.int32),
             pltpu.VMEM((TILE, TILE * PORTALS), jnp.bfloat16),
             pltpu.VMEM((1, 1, PORTALS), jnp.int32),
-            pltpu.VMEM((TILE, TILE * PORTALS), jnp.bfloat16),
-            pltpu.VMEM((1, 1, PORTALS, PORTALS), jnp.float32),
+            pltpu.SMEM((1, 1, PORTALS), jnp.int32),
             pltpu.VMEM((TILE, LANES), jnp.int32),
             pltpu.VMEM((2, STRIP, LANES), jnp.int32),
             pltpu.VMEM((8, STRIP, LANES), jnp.int32),
             pltpu.VMEM((2, TILE + 2 * STRIP, LANES), jnp.float32),
             pltpu.VMEM((EXT, LANES), jnp.float32),
-            pltpu.VMEM((GROUPS, EXT, LANES), jnp.float32),
+            pltpu.VMEM((OWN, EXT, LANES), jnp.float32),
+            pltpu.VMEM((2, 2, TILE, LANES), jnp.float32),
+            pltpu.VMEM((2, 2, EXT, LANES), jnp.float32),
             pltpu.VMEM((GROUPS, STEP, 8, LANES), jnp.float32),
             pltpu.VMEM((GROUPS, STEP, 8, LANES), jnp.float32),
             pltpu.VMEM((PORTALS, LANES), jnp.float32),
@@ -374,8 +442,7 @@
             pltpu.VMEM((2, 8, LANES), jnp.float32),
             pltpu.VMEM((6, 8, LANES), jnp.float32),
             pltpu.VMEM((12, PORTALS, LANES), jnp.float32),
-            pltpu.SemaphoreType.DMA((4,)),
-            pltpu.SemaphoreType.DMA((2,)),
+            pltpu.SemaphoreType.DMA((7,)),
             pltpu.SemaphoreType.DMA((8,)),
             pltpu.SemaphoreType.DMA((8,)),
             pltpu.SemaphoreType.DMA((8,)),
@@ -386,7 +453,7 @@
         compiler_params=pltpu.CompilerParams(
             collective_id=0, has_side_effects=True, vmem_limit_bytes=16 * 2**20
         ),
-    )(portal_index, heights, blocked, estimate, portal_index)
+    )(heights, blocked, estimate, portal_index)
 
 
 def solution(mesh):

time: 43.1 us -> 33.4 us (0.77)
  Pallas kernels: 37.7 us -> 28 us
    pallas_call x1, Pallas kernels: 37.7 us -> 28 us  [body(): pl.pallas_call(kernel, out_shape=(jax.ShapeDtypeStruct(estimate.shape, jn...]
where the time goes in v2:
time: 33.4 us; the launch traced here: 33.1 us
  Pallas kernels  28 us (84%)
  local copies, waits for them, and re-layouts  4.42 us (13%)
  between operations  0.65 us (2%)
    pallas_call x1, Pallas kernels, body(): pl.pallas_call(kernel, out_shape=(jax.ShapeDtypeStruct(estimate.shape, jn...  28 us
    unnamed x10, local copies, waits for them, and re-layouts  4.42 us

profile of v2, /device:TPU:8, one launch (start us, length us, event | category | flops | bytes accessed | tf_op | source)
XLA Modules:
  0.0 33.1 jit_solution(3453688205358796932)
XLA Ops:
  0.6 0.0 copy-start
  0.6 0.9 %copy-done = bf16[64,2048]{1,0:T(8,128)(2,1)S(1)} copy-done((bf16[64,2048]{1,0:T(8,128)(2,1)S(1)}, bf16[64,2048]{1,0:T(8,128)(2,1)}, u32[]{:S(2)}) %copy-start) | copy-done | bytes 262168
  1.6 0.0 copy-start.1
  1.6 0.8 %copy-done.1 = s32[64,64]{1,0:T(8,128)S(1)} copy-done((s32[64,64]{1,0:T(8,128)S(1)}, s32[64,64]{1,0:T(8,128)}, u32[]{:S(2)}) %copy-start.1) | copy-done | bytes 16408
  2.3 0.0 copy-start.2
  2.3 0.8 %copy-done.2 = s32[64,64]{1,0:T(8,128)S(1)} copy-done((s32[64,64]{1,0:T(8,128)S(1)}, s32[64,64]{1,0:T(8,128)}, u32[]{:S(2)}) %copy-start.2) | copy-done | bytes 16408
  3.1 0.0 copy-start.3
  3.1 0.7 %copy-done.3 = s32[1,1,32]{2,1,0:T(1,128)S(1)} copy-done((s32[1,1,32]{2,1,0:T(1,128)S(1)}, s32[1,1,32]{2,1,0:T(1,128)}, u32[]{:S(2)}) %copy-start.3) | copy-done | bytes 152
  3.8 28.0 %shard_map.59 = (bf16[64,2048]{1,0:T(8,128)(2,1)S(1)}, f32[1,1,32,32]{3,2,1,0:T(8,128)S(1)}) custom-call(s32[64,64]{1,0:T(8,128)S(1)} %copy-done.1, s32[64,64]{1,0:T(8,128)S(1)} %copy-done.2, bf16[64,2048]{1,0:T(8,128)(2,1)S(1)} %copy-done, s32[1,1,32]{2,1,0:T(1,128)S(1)} %copy-done.3), custom_call_target="tpu_custom_call" | custom-call | tf_op jit(solution)/shard_map/pallas_call | solution.py:416
  31.8 0.7 %copy.8 = bf16[64,2048]{1,0:T(8,128)(2,1)} copy(bf16[64,2048]{1,0:T(8,128)(2,1)S(1)} %get-tuple-element.4) | data formatting | bytes 524288
  32.5 0.6 %copy.9 = f32[1,1,32,32]{3,2,1,0:T(8,128)} copy(f32[1,1,32,32]{3,2,1,0:T(8,128)S(1)} %get-tuple-element.5) | data formatting | bytes 8192
Async XLA Ops:
  0.6 1.0 %copy-start = (bf16[64,2048]{1,0:T(8,128)(2,1)S(1)}, bf16[64,2048]{1,0:T(8,128)(2,1)}, u32[]{:S(2)}) copy-start(bf16[64,2048]{1,0:T(8,128)(2,1)} %estimate_hbm.1) | copy-start | bytes 786436
  1.6 0.8 %copy-start.1 = (s32[64,64]{1,0:T(8,128)S(1)}, s32[64,64]{1,0:T(8,128)}, u32[]{:S(2)}) copy-start(s32[64,64]{1,0:T(8,128)} %heights_hbm.1) | copy-start | bytes 49156
  2.3 0.8 %copy-start.2 = (s32[64,64]{1,0:T(8,128)S(1)}, s32[64,64]{1,0:T(8,128)}, u32[]{:S(2)}) copy-start(s32[64,64]{1,0:T(8,128)} %blocked_hbm.1) | copy-start | bytes 49156
  3.1 0.7 %copy-start.3 = (s32[1,1,32]{2,1,0:T(1,128)S(1)}, s32[1,1,32]{2,1,0:T(1,128)}, u32[]{:S(2)}) copy-start(s32[1,1,32]{2,1,0:T(1,128)} %portal_hbm.1) | copy-start | bytes 388

commit v3 on v2

--- a/solution.py
+++ b/solution.py
@@ -21,7 +21,7 @@
 FAR = 1000000.0
 
 
-AROUND = ((-1, 0), (1, 0), (0, -1), (0, 1), (-1, -1), (-1, 1), (1, -1), (1, 1))
+AROUND = ((-1, -1), (-1, 1), (1, -1), (1, 1), (-1, 0), (1, 0), (0, -1), (0, 1))
 
 
 def lane_take(values, index):
@@ -347,7 +347,7 @@
                 table.at[level], table_in.at[3 * level + at],
                 table_send.at[3 * level + at], table_recv.at[3 * level + at], device,
             )
-            for at, device in enumerate(partners[level])
+            for at, device in reversed(tuple(enumerate(partners[level])))
         ]
         table_copies.extend(copies)
         return copies
@@ -410,15 +410,27 @@
         copy.wait_send()
 
 
+def hand_out(relaxed_in, merged_in, relaxed, merged, sem):
+    copies = [
+        pltpu.make_async_copy(relaxed_in, relaxed, sem.at[0]),
+        pltpu.make_async_copy(merged_in, merged, sem.at[1]),
+    ]
+    for copy in copies:
+        copy.start()
+    for copy in copies:
+        copy.wait()
+
+
 def body(heights, blocked, estimate, portal_index):
     in_hbm = pl.BlockSpec(memory_space=pltpu.HBM)
     in_vmem = pl.BlockSpec(memory_space=pltpu.VMEM)
-    return pl.pallas_call(
+    outs = (
+        jax.ShapeDtypeStruct(estimate.shape, jnp.bfloat16),
+        jax.ShapeDtypeStruct((1, 1, PORTALS, PORTALS), jnp.float32),
+    )
+    results = pl.pallas_call(
         kernel,
-        out_shape=(
-            jax.ShapeDtypeStruct(estimate.shape, jnp.bfloat16),
-            jax.ShapeDtypeStruct((1, 1, PORTALS, PORTALS), jnp.float32),
-        ),
+        out_shape=outs,
         in_specs=[in_hbm] * 4,
         out_specs=(in_vmem, in_vmem),
         scratch_shapes=[
@@ -453,7 +465,15 @@
         compiler_params=pltpu.CompilerParams(
             collective_id=0, has_side_effects=True, vmem_limit_bytes=16 * 2**20
         ),
-    )(heights, blocked, estimate, portal_index)
+    )(*(pltpu.with_memory_space_constraint(x, pltpu.HBM) for x in (heights, blocked, estimate, portal_index)))
+    return pl.pallas_call(
+        hand_out,
+        out_shape=tuple(pltpu.HBM(x.shape, x.dtype) for x in outs),
+        in_specs=[in_vmem] * 2,
+        out_specs=[in_hbm] * 2,
+        scratch_shapes=[pltpu.SemaphoreType.DMA((2,))],
+        compiler_params=pltpu.CompilerParams(vmem_limit_bytes=2**20),
+    )(*(pltpu.with_memory_space_constraint(x, pltpu.VMEM) for x in results))
 
 
 def solution(mesh):

time: 33.4 us -> 28.6 us (0.86)
  local copies, waits for them, and re-layouts: 4.42 us -> 0 us
    unnamed x10 -> x0, local copies, waits for them, and re-layouts: 4.42 us -> none
    pallas_call x1 -> x2, Pallas kernels: 28 us -> 27.8 us  [the longest x1 27.1 us: body(): pl.pallas_call(kernel, out_shape=outs, in_specs=[in_hbm] * 4, out_specs=(...]
where the time goes in v3:
time: 28.6 us; the launch traced here: 28.4 us
  Pallas kernels  27.8 us (97%)
  between operations  0.64 us (2%)
    pallas_call x1, Pallas kernels, body(): pl.pallas_call(kernel, out_shape=outs, in_specs=[in_hbm] * 4, out_specs=(...  27.1 us
    pallas_call x1, Pallas kernels, body(): pl.pallas_call(hand_out, out_shape=tuple((pltpu.HBM(x.shape, x.dtype) for...  0.72 us

profile of v3, /device:TPU:8, one launch (start us, length us, event | category | flops | bytes accessed | tf_op | source)
XLA Modules:
  0.0 28.4 jit_solution(6066545504404258351)
XLA Ops:
  0.6 27.1 %shard_map.59 = (bf16[64,2048]{1,0:T(8,128)(2,1)S(1)}, f32[1,1,32,32]{3,2,1,0:T(8,128)S(1)}) custom-call(s32[64,64]{1,0:T(8,128)} %heights_hbm.1, s32[64,64]{1,0:T(8,128)} %blocked_hbm.1, bf16[64,2048]{1,0:T(8,128)(2,1)} %estimate_hbm.1, s32[1,1,32]{2,1,0:T(1,128)} %portal_hbm.1), custom_call_target="tpu_custom_call" | custom-call | tf_op jit(solution)/shard_map/pallas_call | solution.py:431
  27.7 0.7 %shard_map.60 = (bf16[64,2048]{1,0:T(8,128)(2,1)}, f32[1,1,32,32]{3,2,1,0:T(8,128)}) custom-call(bf16[64,2048]{1,0:T(8,128)(2,1)S(1)} %get-tuple-element.4.relaxed_in, f32[1,1,32,32]{3,2,1,0:T(8,128)S(1)} %get-tuple-element.5.merged_in), custom_call_target="tpu_custom_call" | custom-call | tf_op jit(solution)/shard_map/pallas_call | solution.py:469

commit v4 on v3

--- a/solution.py
+++ b/solution.py
@@ -267,12 +267,20 @@
         for group in range(GROUPS):
             cost[group, at] = lane_take(values, first_column + (group if group < OWN else group - OWN + halo_shift))
 
+    loads[6].wait()
+    cells = [portal_smem[0, 0, at] for at in range(PORTALS)]
+    for at, cell in enumerate(cells):
+        shifts[at : at + 1, :] = jnp.full((1, LANES), ((cell >> 4) & (BLOCKS - 1)) * PORTALS, jnp.int32)
+
     for copy in field_copies:
         copy.wait_recv()
 
+    def half_cost(group, at):
+        here = cost[group, at]
+        return jnp.where(here >= FAR, FAR, 0.5 * here)
+
     def start(group, at, distance):
-        here = cost[group, at]
-        dist[group, at] = jnp.where(here >= FAR, FAR, distance + 0.5 * here)
+        dist[group, at] = jnp.minimum(distance + half_cost(group, at), FAR)
 
     for at in range(STEP):
         for group in range(OWN):
@@ -327,12 +335,8 @@
         for at in range(STEP):
             field[group, pl.ds(at, 8, stride=STEP), :] = dist[group, at] - 0.5 * cost[group, at]
 
-    loads[6].wait()
-    for at in range(PORTALS):
-        cell = portal_smem[0, 0, at]
-        column_at = cell % TILE
-        rows[at : at + 1, :] = field[column_at % OWN, pl.ds(HALO + cell // TILE, 1), :]
-        shifts[at : at + 1, :] = jnp.full((1, LANES), column_at // OWN * PORTALS, jnp.int32)
+    for at, cell in enumerate(cells):
+        rows[at : at + 1, :] = field[cell & (OWN - 1), pl.ds(HALO + (cell >> 6), 1), :]
     first = jnp.zeros((8, LANES), jnp.float32)
     for part in range(4):
         index = shifts[part * 8 : part * 8 + 8, :] + lane_class
@@ -349,8 +353,7 @@
             )
             for at, device in reversed(tuple(enumerate(partners[level])))
         ]
-        table_copies.extend(copies)
-        return copies
+        table_copies.extend(reversed(copies))
 
     def left_of(values):
         return [lane_take(values, lane_block * PORTALS + at) for at in range(PORTALS)]
@@ -390,16 +393,21 @@
 
     now = first
     for level in range(2):
-        copies = exchange(level)
+        exchange(level)
         now_left, now_right = left_of(now), right_of(now, 6 * level)
         relax_out(2 * level)
         relax_out(2 * level + 1)
-        for copy in copies:
-            copy.wait_recv()
-        by_row, by_col, by_both = (table_in[3 * level + at] for at in range(3))
+        def arrived(at):
+            table_copies[3 * level + at].wait_recv()
+            return table_in[3 * level + at]
+
+        by_col = arrived(1)
+        col_left, col_right = left_of(by_col), right_of(by_col, 6 * level + 2)
+        by_row = arrived(0)
         here = pair(now, now_left, now_right, right_of(by_row, 6 * level + 1))
-        there = pair(by_col, left_of(by_col), right_of(by_col, 6 * level + 2), right_of(by_both, 6 * level + 3))
-        now = pair(here, left_of(here), right_of(here, 6 * level + 4), right_of(there, 6 * level + 5))
+        here_left, here_right = left_of(here), right_of(here, 6 * level + 4)
+        there = pair(by_col, col_left, col_right, right_of(arrived(2), 6 * level + 3))
+        now = pair(here, here_left, here_right, right_of(there, 6 * level + 5))
         if level == 0:
             table[1] = now
     now = now * 0.0625

time: 28.6 us -> 28.7 us (level)
  no operation moved by 1% of the time
where the time goes in v4:
time: 28.7 us; the launch traced here: 28.5 us
  Pallas kernels  27.9 us (97%)
  between operations  0.64 us (2%)
    pallas_call x1, Pallas kernels, body(): pl.pallas_call(kernel, out_shape=outs, in_specs=[in_hbm] * 4, out_specs=(...  27.2 us
    pallas_call x1, Pallas kernels, body(): pl.pallas_call(hand_out, out_shape=tuple((pltpu.HBM(x.shape, x.dtype) for...  0.72 us

profile of v4, /device:TPU:8, one launch (start us, length us, event | category | flops | bytes accessed | tf_op | source)
XLA Modules:
  0.0 28.5 jit_solution(13475006805452128837)
XLA Ops:
  0.6 27.2 %shard_map.59 = (bf16[64,2048]{1,0:T(8,128)(2,1)S(1)}, f32[1,1,32,32]{3,2,1,0:T(8,128)S(1)}) custom-call(s32[64,64]{1,0:T(8,128)} %heights_hbm.1, s32[64,64]{1,0:T(8,128)} %blocked_hbm.1, bf16[64,2048]{1,0:T(8,128)(2,1)} %estimate_hbm.1, s32[1,1,32]{2,1,0:T(1,128)} %portal_hbm.1), custom_call_target="tpu_custom_call" | custom-call | tf_op jit(solution)/shard_map/pallas_call | solution.py:439
  27.8 0.7 %shard_map.60 = (bf16[64,2048]{1,0:T(8,128)(2,1)}, f32[1,1,32,32]{3,2,1,0:T(8,128)}) custom-call(bf16[64,2048]{1,0:T(8,128)(2,1)S(1)} %get-tuple-element.4.relaxed_in, f32[1,1,32,32]{3,2,1,0:T(8,128)S(1)} %get-tuple-element.5.merged_in), custom_call_target="tpu_custom_call" | custom-call | tf_op jit(solution)/shard_map/pallas_call | solution.py:477

commit v5 on v4

--- a/solution.py
+++ b/solution.py
@@ -46,16 +46,16 @@
     def other(index, bit):
         return index + bit - 2 * bit * lax.rem(index // bit, 2)
 
-    partners = []
-    for level in range(2):
-        bit = 1 << level
-        partners.append(
-            [
-                (other(row_index, bit), col_index),
-                (row_index, other(col_index, bit)),
-                (other(row_index, bit), other(col_index, bit)),
-            ]
-        )
+    def partner(index, step):
+        for bit in (1, 2):
+            if step & bit:
+                index = other(index, bit)
+        return index
+
+    steps = [(a, b) for a in range(4) for b in range(4) if a or b]
+    blocks = {(a, b): 2 * (a // 2) + b // 2 for a, b in steps}
+    steps.sort(key=lambda step: (0, 3, 2, 1).index(blocks[step]))
+    partners = {(a, b): (partner(row_index, a), partner(col_index, b)) for a, b in steps}
 
     loads = [
         pltpu.make_async_copy(source, target, load_sem.at[at])
@@ -75,7 +75,7 @@
         load.start()
 
     barrier = pltpu.get_barrier_semaphore()
-    met = around + partners[1]
+    met = around + [partners[step] for step in steps if max(step) > 1]
     for device in met:
         pl.semaphore_signal(barrier, inc=1, device_id=device, device_id_type=pl.DeviceIdType.MESH)
 
@@ -265,7 +265,9 @@
     for at in range(STEP):
         values = cost_rows[pl.ds(at, 8, stride=STEP), :]
         for group in range(GROUPS):
-            cost[group, at] = lane_take(values, first_column + (group if group < OWN else group - OWN + halo_shift))
+            here = lane_take(values, first_column + (group if group < OWN else group - OWN + halo_shift))
+            cost[group, at] = here
+            dist[group, at] = jnp.where(here >= FAR, FAR, 0.5 * here)
 
     loads[6].wait()
     cells = [portal_smem[0, 0, at] for at in range(PORTALS)]
@@ -275,12 +277,8 @@
     for copy in field_copies:
         copy.wait_recv()
 
-    def half_cost(group, at):
-        here = cost[group, at]
-        return jnp.where(here >= FAR, FAR, 0.5 * here)
-
     def start(group, at, distance):
-        dist[group, at] = jnp.minimum(distance + half_cost(group, at), FAR)
+        dist[group, at] = jnp.minimum(distance + dist[group, at], FAR)
 
     for at in range(STEP):
         for group in range(OWN):
@@ -341,24 +339,23 @@
     for part in range(4):
         index = shifts[part * 8 : part * 8 + 8, :] + lane_class
         first = jnp.where(lane_block == part, lane_take(rows[part * 8 : part * 8 + 8, :], index), first)
-    table[0] = first
-
-    table_copies = []
-
-    def exchange(level):
-        copies = [
-            send(
-                table.at[level], table_in.at[3 * level + at],
-                table_send.at[3 * level + at], table_recv.at[3 * level + at], device,
-            )
-            for at, device in reversed(tuple(enumerate(partners[level])))
-        ]
-        table_copies.extend(reversed(copies))
+    table[...] = first
+
+    table_copies = {
+        (a, b): send(
+            table, table_in.at[4 * a + b], table_send.at[4 * a + b], table_recv.at[4 * a + b], partners[a, b]
+        )
+        for a, b in steps
+    }
 
     def left_of(values):
         return [lane_take(values, lane_block * PORTALS + at) for at in range(PORTALS)]
 
-    def right_of(values, slot):
+    slots_used = []
+
+    def right_of(values):
+        slot = len(slots_used)
+        slots_used.append(slot)
         for part in range(4):
             right_rows[slot, part * 8 : part * 8 + 8, :] = lane_take(values, lane_class + part * PORTALS)
         return [
@@ -371,9 +368,13 @@
             sums = [jnp.minimum(a, b) for a, b in zip(sums[::2], sums[1::2])]
         return sums[0]
 
-    def pair(near_table, near_left, near_right, far_right):
-        through = minplus(near_left, far_right)
-        return jnp.minimum(near_table, minplus(left_of(through), near_right))
+    def sides(values):
+        return values, left_of(values), right_of(values)
+
+    def pair(near, far_table):
+        values, near_left, near_right = near
+        through = minplus(near_left, right_of(far_table))
+        return jnp.minimum(values, minplus(left_of(through), near_right))
 
     def relax_out(part):
         for first_at in range(4):
@@ -391,30 +392,29 @@
                 values = jnp.concatenate([for_rows[0][at], for_rows[1][at]], axis=0)
                 relaxed[part * 16 : part * 16 + 16, group * LANES : (group + 1) * LANES] = values.astype(jnp.bfloat16)
 
-    now = first
-    for level in range(2):
-        exchange(level)
-        now_left, now_right = left_of(now), right_of(now, 6 * level)
-        relax_out(2 * level)
-        relax_out(2 * level + 1)
-        def arrived(at):
-            table_copies[3 * level + at].wait_recv()
-            return table_in[3 * level + at]
-
-        by_col = arrived(1)
-        col_left, col_right = left_of(by_col), right_of(by_col, 6 * level + 2)
-        by_row = arrived(0)
-        here = pair(now, now_left, now_right, right_of(by_row, 6 * level + 1))
-        here_left, here_right = left_of(here), right_of(here, 6 * level + 4)
-        there = pair(by_col, col_left, col_right, right_of(arrived(2), 6 * level + 3))
-        now = pair(here, here_left, here_right, right_of(there, 6 * level + 5))
-        if level == 0:
-            table[1] = now
+    def arrived(a, b):
+        table_copies[a, b].wait_recv()
+        return table_in[4 * a + b]
+
+    def block(a, b):
+        near, beside = sides(arrived(a, b)), sides(arrived(a, b + 1))
+        below, across = arrived(a + 1, b), arrived(a + 1, b + 1)
+        return pair(sides(pair(near, below)), pair(beside, across))
+
+    near = sides(first)
+    for part in range(4):
+        relax_out(part)
+    beside = sides(arrived(0, 1))
+    beside = pair(beside, arrived(1, 1))
+    second = sides(pair(sides(pair(near, arrived(1, 0))), beside))
+    third = sides(pair(second, block(2, 0)))
+    beside = sides(block(0, 2))
+    now = pair(third, pair(beside, block(2, 2)))
     now = now * 0.0625
     for part in range(4):
         merged[0, 0, part * 8 : part * 8 + 8, :] = now[:, part * PORTALS : (part + 1) * PORTALS]
 
-    for copy in ground_copies + table_copies:
+    for copy in ground_copies + list(table_copies.values()):
         copy.wait_send()
 
 
@@ -459,16 +459,16 @@
             pltpu.VMEM((GROUPS, STEP, 8, LANES), jnp.float32),
             pltpu.VMEM((PORTALS, LANES), jnp.float32),
             pltpu.VMEM((PORTALS, LANES), jnp.int32),
-            pltpu.VMEM((2, 8, LANES), jnp.float32),
-            pltpu.VMEM((6, 8, LANES), jnp.float32),
-            pltpu.VMEM((12, PORTALS, LANES), jnp.float32),
+            pltpu.VMEM((8, LANES), jnp.float32),
+            pltpu.VMEM((16, 8, LANES), jnp.float32),
+            pltpu.VMEM((32, PORTALS, LANES), jnp.float32),
             pltpu.SemaphoreType.DMA((7,)),
             pltpu.SemaphoreType.DMA((8,)),
             pltpu.SemaphoreType.DMA((8,)),
             pltpu.SemaphoreType.DMA((8,)),
             pltpu.SemaphoreType.DMA((8,)),
-            pltpu.SemaphoreType.DMA((6,)),
-            pltpu.SemaphoreType.DMA((6,)),
+            pltpu.SemaphoreType.DMA((16,)),
+            pltpu.SemaphoreType.DMA((16,)),
         ],
         compiler_params=pltpu.CompilerParams(
             collective_id=0, has_side_effects=True, vmem_limit_bytes=16 * 2**20

time: 28.7 us -> 30.8 us (1.073)
  the two profiles are of different devices: /device:TPU:8 before, /device:TPU:1 now
where the time goes in v5:
time: 30.8 us; the launch traced here: 30.7 us
  Pallas kernels  30.1 us (98%)
  between operations  0.64 us (2%)
    pallas_call x1, Pallas kernels, body(): pl.pallas_call(kernel, out_shape=outs, in_specs=[in_hbm] * 4, out_specs=(...  29.3 us
    pallas_call x1, Pallas kernels, body(): pl.pallas_call(hand_out, out_shape=tuple((pltpu.HBM(x.shape, x.dtype) for...  0.72 us

profile of v5, /device:TPU:1, one launch (start us, length us, event | category | flops | bytes accessed | tf_op | source)
XLA Modules:
  0.0 30.7 jit_solution(9023385754272430752)
XLA Ops:
  0.6 29.3 %shard_map.59 = (bf16[64,2048]{1,0:T(8,128)(2,1)S(1)}, f32[1,1,32,32]{3,2,1,0:T(8,128)S(1)}) custom-call(s32[64,64]{1,0:T(8,128)} %heights_hbm.1, s32[64,64]{1,0:T(8,128)} %blocked_hbm.1, bf16[64,2048]{1,0:T(8,128)(2,1)} %estimate_hbm.1, s32[1,1,32]{2,1,0:T(1,128)} %portal_hbm.1), custom_call_target="tpu_custom_call" | custom-call | tf_op jit(solution)/shard_map/pallas_call | solution.py:439
  30.0 0.7 %shard_map.60 = (bf16[64,2048]{1,0:T(8,128)(2,1)}, f32[1,1,32,32]{3,2,1,0:T(8,128)}) custom-call(bf16[64,2048]{1,0:T(8,128)(2,1)S(1)} %get-tuple-element.4.relaxed_in, f32[1,1,32,32]{3,2,1,0:T(8,128)S(1)} %get-tuple-element.5.merged_in), custom_call_target="tpu_custom_call" | custom-call | tf_op jit(solution)/shard_map/pallas_call | solution.py:477

commit v6 on v4

--- a/solution.py
+++ b/solution.py
@@ -57,6 +57,11 @@
             ]
         )
 
+    barrier = pltpu.get_barrier_semaphore()
+    met = around
+    for device in met:
+        pl.semaphore_signal(barrier, inc=1, device_id=device, device_id_type=pl.DeviceIdType.MESH)
+
     loads = [
         pltpu.make_async_copy(source, target, load_sem.at[at])
         for at, (source, target) in enumerate(
@@ -73,11 +78,6 @@
     ]
     for load in loads:
         load.start()
-
-    barrier = pltpu.get_barrier_semaphore()
-    met = around + partners[1]
-    for device in met:
-        pl.semaphore_signal(barrier, inc=1, device_id=device, device_id_type=pl.DeviceIdType.MESH)
 
     def send(source, target, send_sem, recv_sem, device):
         copy = pltpu.make_async_remote_copy(
@@ -111,21 +111,6 @@
     strips[0] = west
     strips[1] = east
 
-    pl.semaphore_wait(barrier, len(met))
-
-    top, bottom = ground.at[0:STRIP], ground.at[TILE - STRIP : TILE]
-    ground_source = {-1: top, 1: bottom}
-    ground_copies = []
-    for at, (dr, dc) in enumerate(AROUND):
-        if dr:
-            source = ground_source[dr]
-        else:
-            source = strips.at[0 if dc < 0 else 1]
-        slot = AROUND.index((-dr, -dc))
-        ground_copies.append(
-            send(source, ground_in.at[slot], ground_send.at[at], ground_recv.at[slot], around[at])
-        )
-
     loads[2].wait()
     own = jnp.broadcast_to(portal[0, 0:1, :], (8, PORTALS))
     portal_cells = jnp.concatenate([own] * BLOCKS, axis=1)
@@ -183,6 +168,21 @@
     prepare(3)
     for part in range(4):
         edges(part)
+
+    pl.semaphore_wait(barrier, len(met))
+
+    top, bottom = ground.at[0:STRIP], ground.at[TILE - STRIP : TILE]
+    ground_source = {-1: top, 1: bottom}
+    ground_copies = []
+    for at, (dr, dc) in enumerate(AROUND):
+        if dr:
+            source = ground_source[dr]
+        else:
+            source = strips.at[0 if dc < 0 else 1]
+        slot = AROUND.index((-dr, -dc))
+        ground_copies.append(
+            send(source, ground_in.at[slot], ground_send.at[at], ground_recv.at[slot], around[at])
+        )
 
     field_copies = []
     for at, (dr, dc) in enumerate(AROUND):

time: 28.7 us -> 28.7 us (level)
  no operation moved by 1% of the time
where the time goes in v6:
time: 28.7 us; the launch traced here: 28.6 us
  Pallas kernels  28 us (98%)
  between operations  0.64 us (2%)
    pallas_call x1, Pallas kernels, body(): pl.pallas_call(kernel, out_shape=outs, in_specs=[in_hbm] * 4, out_specs=(...  27.2 us
    pallas_call x1, Pallas kernels, body(): pl.pallas_call(hand_out, out_shape=tuple((pltpu.HBM(x.shape, x.dtype) for...  0.72 us

profile of v6, /device:TPU:8, one launch (start us, length us, event | category | flops | bytes accessed | tf_op | source)
XLA Modules:
  0.0 28.6 jit_solution(2073580363290001044)
XLA Ops:
  0.6 27.2 %shard_map.59 = (bf16[64,2048]{1,0:T(8,128)(2,1)S(1)}, f32[1,1,32,32]{3,2,1,0:T(8,128)S(1)}) custom-call(s32[64,64]{1,0:T(8,128)} %heights_hbm.1, s32[64,64]{1,0:T(8,128)} %blocked_hbm.1, bf16[64,2048]{1,0:T(8,128)(2,1)} %estimate_hbm.1, s32[1,1,32]{2,1,0:T(1,128)} %portal_hbm.1), custom_call_target="tpu_custom_call" | custom-call | tf_op jit(solution)/shard_map/pallas_call | solution.py:439
  27.9 0.7 %shard_map.60 = (bf16[64,2048]{1,0:T(8,128)(2,1)}, f32[1,1,32,32]{3,2,1,0:T(8,128)}) custom-call(bf16[64,2048]{1,0:T(8,128)(2,1)S(1)} %get-tuple-element.4.relaxed_in, f32[1,1,32,32]{3,2,1,0:T(8,128)S(1)} %get-tuple-element.5.merged_in), custom_call_target="tpu_custom_call" | custom-call | tf_op jit(solution)/shard_map/pallas_call | solution.py:477

commit v7 on v6

--- a/solution.py
+++ b/solution.py
@@ -259,7 +259,7 @@
         (grid_row >= 0) & (grid_row < row_count * TILE)
         & (grid_col >= 0) & (grid_col < col_count * TILE)
     )
-    cost_rows[...] = jnp.where(inside, step_cost, FAR)
+    cost_rows[...] = jnp.where(inside, step_cost, 2.0 * FAR)
     first_column = STRIP + lane_block * OWN
     halo_shift = jnp.where(low, TILE + 4 * lane_block, 4 * lane_block - 16) - lane_block * OWN
     for at in range(STEP):
@@ -275,30 +275,29 @@
     for copy in field_copies:
         copy.wait_recv()
 
-    def half_cost(group, at):
-        here = cost[group, at]
-        return jnp.where(here >= FAR, FAR, 0.5 * here)
-
-    def start(group, at, distance):
-        dist[group, at] = jnp.minimum(distance + half_cost(group, at), FAR)
+    def started(group, at, distance):
+        return jnp.minimum(distance + 0.5 * cost[group, at], FAR)
 
     for at in range(STEP):
-        for group in range(OWN):
-            start(group, at, field[group, pl.ds(at, 8, stride=STEP), :])
         for piece in range(2):
             from_east = side_in[0, piece, pl.ds(at, 8, stride=STEP), :]
             from_west = side_in[1, piece, pl.ds(at, 8, stride=STEP), :]
-            start(OWN + piece, at, jnp.where(low, from_east, from_west))
-            start(OWN + piece + 2, at, pltpu.roll(jnp.where(low, from_west, from_east), 64, 1))
+            for group, values in (
+                (OWN + piece, jnp.where(low, from_east, from_west)),
+                (OWN + piece + 2, pltpu.roll(jnp.where(low, from_west, from_east), 64, 1)),
+            ):
+                dist[group, at] = started(group, at, values)
 
     first_block, last_block = lane_block == 0, lane_block == BLOCKS - 1
 
-    def sweep(_, carry):
+    def sweep(first, last):
         def pairs_of(here, east_of):
             below = east_of[1:] + [pltpu.roll(east_of[0], 7, 0)]
             return [jnp.minimum(a, b) for a, b in zip(here, below)]
 
         def column(group):
+            if first and group < OWN:
+                return [started(group, at, field[group, pl.ds(at, 8, stride=STEP), :]) for at in range(STEP)]
             return [dist[group, at] for at in range(STEP)]
 
         own_first, halo_first = column(0), column(OWN)
@@ -313,6 +312,8 @@
         own_west = [pltpu.roll(jnp.where(last_block, a, b), PORTALS, 1) for a, b in zip(halo_pairs, own_pairs)]
         halo_west = [pltpu.roll(jnp.where(last_block, a, b), PORTALS, 1) for a, b in zip(own_pairs, halo_pairs)]
         for begin, end, west_of, end_pairs in ((0, OWN, own_west, own_pairs), (OWN, GROUPS, halo_west, halo_pairs)):
+            if last and begin == OWN:
+                continue
             now = own_first if begin == 0 else column(begin)
             for group in range(begin, end):
                 if group < end - 1:
@@ -322,18 +323,23 @@
                     pairs = end_pairs
                 north = [pltpu.roll(pairs[STEP - 1], 1, 0)] + pairs[:-1]
                 for at in range(STEP):
-                    nearest = cost[group, at] + jnp.minimum(north[at], west_of[at])
-                    dist[group, at] = jnp.minimum(now[at], nearest)
+                    here = cost[group, at]
+                    shortest = jnp.minimum(now[at], here + jnp.minimum(north[at], west_of[at]))
+                    if last:
+                        field[group, pl.ds(at, 8, stride=STEP), :] = shortest - 0.5 * here
+                    else:
+                        dist[group, at] = shortest
                 west_of, now = pairs, later
+
+    sweep(True, False)
+    def middle(_, carry):
+        sweep(False, False)
         return carry
 
-    lax.fori_loop(0, SWEEPS, sweep, 0)
-
+    lax.fori_loop(0, SWEEPS - 2, middle, 0)
     for copy in field_copies:
         copy.wait_send()
-    for group in range(OWN):
-        for at in range(STEP):
-            field[group, pl.ds(at, 8, stride=STEP), :] = dist[group, at] - 0.5 * cost[group, at]
+    sweep(False, True)
 
     for at, cell in enumerate(cells):
         rows[at : at + 1, :] = field[cell & (OWN - 1), pl.ds(HALO + (cell >> 6), 1), :]

time: 28.7 us -> 28.4 us (0.990)
  Pallas kernels: 28 us -> 27.7 us
    pallas_call x1, Pallas kernels: 27.2 us -> 26.9 us  [body(): pl.pallas_call(kernel, out_shape=outs, in_specs=[in_hbm] * 4, out_specs=(...]
where the time goes in v7:
time: 28.4 us; the launch traced here: 28.3 us
  Pallas kernels  27.7 us (98%)
  between operations  0.64 us (2%)
    pallas_call x1, Pallas kernels, body(): pl.pallas_call(kernel, out_shape=outs, in_specs=[in_hbm] * 4, out_specs=(...  26.9 us
    pallas_call x1, Pallas kernels, body(): pl.pallas_call(hand_out, out_shape=tuple((pltpu.HBM(x.shape, x.dtype) for...  0.72 us

profile of v7, /device:TPU:8, one launch (start us, length us, event | category | flops | bytes accessed | tf_op | source)
XLA Modules:
  0.0 28.3 jit_solution(17671021994644919749)
XLA Ops:
  0.6 26.9 %shard_map.59 = (bf16[64,2048]{1,0:T(8,128)(2,1)S(1)}, f32[1,1,32,32]{3,2,1,0:T(8,128)S(1)}) custom-call(s32[64,64]{1,0:T(8,128)} %heights_hbm.1, s32[64,64]{1,0:T(8,128)} %blocked_hbm.1, bf16[64,2048]{1,0:T(8,128)(2,1)} %estimate_hbm.1, s32[1,1,32]{2,1,0:T(1,128)} %portal_hbm.1), custom_call_target="tpu_custom_call" | custom-call | tf_op jit(solution)/shard_map/pallas_call | solution.py:445
  27.6 0.7 %shard_map.60 = (bf16[64,2048]{1,0:T(8,128)(2,1)}, f32[1,1,32,32]{3,2,1,0:T(8,128)}) custom-call(bf16[64,2048]{1,0:T(8,128)(2,1)S(1)} %get-tuple-element.4.relaxed_in, f32[1,1,32,32]{3,2,1,0:T(8,128)S(1)} %get-tuple-element.5.merged_in), custom_call_target="tpu_custom_call" | custom-call | tf_op jit(solution)/shard_map/pallas_call | solution.py:483

commit v8 on v7

--- a/solution.py
+++ b/solution.py
@@ -272,8 +272,9 @@
     for at, cell in enumerate(cells):
         shifts[at : at + 1, :] = jnp.full((1, LANES), ((cell >> 4) & (BLOCKS - 1)) * PORTALS, jnp.int32)
 
-    for copy in field_copies:
-        copy.wait_recv()
+    for copy, (_, dc) in zip(field_copies, AROUND):
+        if dc:
+            copy.wait_recv()
 
     def started(group, at, distance):
         return jnp.minimum(distance + 0.5 * cost[group, at], FAR)
@@ -287,6 +288,10 @@
                 (OWN + piece + 2, pltpu.roll(jnp.where(low, from_west, from_east), 64, 1)),
             ):
                 dist[group, at] = started(group, at, values)
+
+    for copy, (_, dc) in zip(field_copies, AROUND):
+        if not dc:
+            copy.wait_recv()
 
     first_block, last_block = lane_block == 0, lane_block == BLOCKS - 1
 
@@ -409,11 +414,16 @@
 
         by_col = arrived(1)
         col_left, col_right = left_of(by_col), right_of(by_col, 6 * level + 2)
+        if level == 0:
+            there = pair(by_col, col_left, col_right, right_of(arrived(2), 6 * level + 3))
+            there_right = right_of(there, 6 * level + 5)
         by_row = arrived(0)
         here = pair(now, now_left, now_right, right_of(by_row, 6 * level + 1))
         here_left, here_right = left_of(here), right_of(here, 6 * level + 4)
-        there = pair(by_col, col_left, col_right, right_of(arrived(2), 6 * level + 3))
-        now = pair(here, here_left, here_right, right_of(there, 6 * level + 5))
+        if level == 1:
+            there = pair(by_col, col_left, col_right, right_of(arrived(2), 6 * level + 3))
+            there_right = right_of(there, 6 * level + 5)
+        now = pair(here, here_left, here_right, there_right)
         if level == 0:
             table[1] = now
     now = now * 0.0625

time: 28.4 us -> 28.1 us (0.989)
  Pallas kernels: 27.7 us -> 27.3 us
    pallas_call x1, Pallas kernels: 26.9 us -> 26.6 us  [body(): pl.pallas_call(kernel, out_shape=outs, in_specs=[in_hbm] * 4, out_specs=(...]
where the time goes in v8:
time: 28.1 us; the launch traced here: 28 us
  Pallas kernels  27.3 us (97%)
  between operations  0.64 us (2%)
    pallas_call x1, Pallas kernels, body(): pl.pallas_call(kernel, out_shape=outs, in_specs=[in_hbm] * 4, out_specs=(...  26.6 us
    pallas_call x1, Pallas kernels, body(): pl.pallas_call(hand_out, out_shape=tuple((pltpu.HBM(x.shape, x.dtype) for...  0.72 us

profile of v8, /device:TPU:8, one launch (start us, length us, event | category | flops | bytes accessed | tf_op | source)
XLA Modules:
  0.0 28.0 jit_solution(5364282132901937828)
XLA Ops:
  0.6 26.6 %shard_map.59 = (bf16[64,2048]{1,0:T(8,128)(2,1)S(1)}, f32[1,1,32,32]{3,2,1,0:T(8,128)S(1)}) custom-call(s32[64,64]{1,0:T(8,128)} %heights_hbm.1, s32[64,64]{1,0:T(8,128)} %blocked_hbm.1, bf16[64,2048]{1,0:T(8,128)(2,1)} %estimate_hbm.1, s32[1,1,32]{2,1,0:T(1,128)} %portal_hbm.1), custom_call_target="tpu_custom_call" | custom-call | tf_op jit(solution)/shard_map/pallas_call | solution.py:455
  27.2 0.7 %shard_map.60 = (bf16[64,2048]{1,0:T(8,128)(2,1)}, f32[1,1,32,32]{3,2,1,0:T(8,128)}) custom-call(bf16[64,2048]{1,0:T(8,128)(2,1)S(1)} %get-tuple-element.4.relaxed_in, f32[1,1,32,32]{3,2,1,0:T(8,128)S(1)} %get-tuple-element.5.merged_in), custom_call_target="tpu_custom_call" | custom-call | tf_op jit(solution)/shard_map/pallas_call | solution.py:493

commit v9 on v8

--- a/solution.py
+++ b/solution.py
@@ -405,6 +405,9 @@
     now = first
     for level in range(2):
         exchange(level)
+        if level == 0:
+            for copy in ground_copies:
+                copy.wait_send()
         now_left, now_right = left_of(now), right_of(now, 6 * level)
         relax_out(2 * level)
         relax_out(2 * level + 1)
@@ -416,21 +419,22 @@
         col_left, col_right = left_of(by_col), right_of(by_col, 6 * level + 2)
         if level == 0:
             there = pair(by_col, col_left, col_right, right_of(arrived(2), 6 * level + 3))
-            there_right = right_of(there, 6 * level + 5)
-        by_row = arrived(0)
-        here = pair(now, now_left, now_right, right_of(by_row, 6 * level + 1))
-        here_left, here_right = left_of(here), right_of(here, 6 * level + 4)
-        if level == 1:
+            there_left = left_of(there)
+            here = pair(now, now_left, now_right, right_of(arrived(0), 6 * level + 1))
+            around_here = minplus(there_left, right_of(here, 6 * level + 4))
+            now = jnp.minimum(here, minplus(left_of(here), right_of(around_here, 6 * level + 5)))
+        else:
+            here = pair(now, now_left, now_right, right_of(arrived(0), 6 * level + 1))
+            here_left, here_right = left_of(here), right_of(here, 6 * level + 4)
             there = pair(by_col, col_left, col_right, right_of(arrived(2), 6 * level + 3))
-            there_right = right_of(there, 6 * level + 5)
-        now = pair(here, here_left, here_right, there_right)
+            now = pair(here, here_left, here_right, right_of(there, 6 * level + 5))
         if level == 0:
             table[1] = now
     now = now * 0.0625
     for part in range(4):
         merged[0, 0, part * 8 : part * 8 + 8, :] = now[:, part * PORTALS : (part + 1) * PORTALS]
 
-    for copy in ground_copies + table_copies:
+    for copy in table_copies:
         copy.wait_send()
 
 

time: 28.1 us -> 28 us (level)
  no operation moved by 1% of the time
where the time goes in v9:
time: 28 us; the launch traced here: 27.8 us
  Pallas kernels  27.2 us (97%)
  between operations  0.64 us (2%)
    pallas_call x1, Pallas kernels, body(): pl.pallas_call(kernel, out_shape=outs, in_specs=[in_hbm] * 4, out_specs=(...  26.5 us
    pallas_call x1, Pallas kernels, body(): pl.pallas_call(hand_out, out_shape=tuple((pltpu.HBM(x.shape, x.dtype) for...  0.72 us

profile of v9, /device:TPU:8, one launch (start us, length us, event | category | flops | bytes accessed | tf_op | source)
XLA Modules:
  0.0 27.8 jit_solution(11255953182488604312)
XLA Ops:
  0.6 26.5 %shard_map.59 = (bf16[64,2048]{1,0:T(8,128)(2,1)S(1)}, f32[1,1,32,32]{3,2,1,0:T(8,128)S(1)}) custom-call(s32[64,64]{1,0:T(8,128)} %heights_hbm.1, s32[64,64]{1,0:T(8,128)} %blocked_hbm.1, bf16[64,2048]{1,0:T(8,128)(2,1)} %estimate_hbm.1, s32[1,1,32]{2,1,0:T(1,128)} %portal_hbm.1), custom_call_target="tpu_custom_call" | custom-call | tf_op jit(solution)/shard_map/pallas_call | solution.py:459
  27.1 0.7 %shard_map.60 = (bf16[64,2048]{1,0:T(8,128)(2,1)}, f32[1,1,32,32]{3,2,1,0:T(8,128)}) custom-call(bf16[64,2048]{1,0:T(8,128)(2,1)S(1)} %get-tuple-element.4.relaxed_in, f32[1,1,32,32]{3,2,1,0:T(8,128)S(1)} %get-tuple-element.5.merged_in), custom_call_target="tpu_custom_call" | custom-call | tf_op jit(solution)/shard_map/pallas_call | solution.py:497

commit v10 on v9

--- a/solution.py
+++ b/solution.py
@@ -339,9 +339,10 @@
     sweep(True, False)
     def middle(_, carry):
         sweep(False, False)
+        sweep(False, False)
         return carry
 
-    lax.fori_loop(0, SWEEPS - 2, middle, 0)
+    lax.fori_loop(0, (SWEEPS - 2) // 2, middle, 0)
     for copy in field_copies:
         copy.wait_send()
     sweep(False, True)

time: 28 us -> 27.9 us (level)
  no operation moved by 1% of the time
where the time goes in v10:
time: 27.9 us; the launch traced here: 27.8 us
  Pallas kernels  27.2 us (97%)
  between operations  0.64 us (2%)
    pallas_call x1, Pallas kernels, body(): pl.pallas_call(kernel, out_shape=outs, in_specs=[in_hbm] * 4, out_specs=(...  26.4 us
    pallas_call x1, Pallas kernels, body(): pl.pallas_call(hand_out, out_shape=tuple((pltpu.HBM(x.shape, x.dtype) for...  0.72 us

profile of v10, /device:TPU:8, one launch (start us, length us, event | category | flops | bytes accessed | tf_op | source)
XLA Modules:
  0.0 27.8 jit_solution(1710546168793419670)
XLA Ops:
  0.6 26.4 %shard_map.59 = (bf16[64,2048]{1,0:T(8,128)(2,1)S(1)}, f32[1,1,32,32]{3,2,1,0:T(8,128)S(1)}) custom-call(s32[64,64]{1,0:T(8,128)} %heights_hbm.1, s32[64,64]{1,0:T(8,128)} %blocked_hbm.1, bf16[64,2048]{1,0:T(8,128)(2,1)} %estimate_hbm.1, s32[1,1,32]{2,1,0:T(1,128)} %portal_hbm.1), custom_call_target="tpu_custom_call" | custom-call | tf_op jit(solution)/shard_map/pallas_call | solution.py:460
  27.1 0.7 %shard_map.60 = (bf16[64,2048]{1,0:T(8,128)(2,1)}, f32[1,1,32,32]{3,2,1,0:T(8,128)}) custom-call(bf16[64,2048]{1,0:T(8,128)(2,1)S(1)} %get-tuple-element.4.relaxed_in, f32[1,1,32,32]{3,2,1,0:T(8,128)S(1)} %get-tuple-element.5.merged_in), custom_call_target="tpu_custom_call" | custom-call | tf_op jit(solution)/shard_map/pallas_call | solution.py:498

commit v11 on v9

--- a/solution.py
+++ b/solution.py
@@ -357,14 +357,15 @@
     table_copies = []
 
     def exchange(level):
+        order = ((2, 1, 0), (2, 0, 1))[level]
         copies = [
             send(
                 table.at[level], table_in.at[3 * level + at],
                 table_send.at[3 * level + at], table_recv.at[3 * level + at], device,
             )
-            for at, device in reversed(tuple(enumerate(partners[level])))
+            for at, device in ((at, partners[level][at]) for at in order)
         ]
-        table_copies.extend(reversed(copies))
+        table_copies.extend(copies[order.index(at)] for at in range(3))
 
     def left_of(values):
         return [lane_take(values, lane_block * PORTALS + at) for at in range(PORTALS)]

time: 28 us -> 28 us (level)
  no operation moved by 1% of the time
where the time goes in v11:
time: 28 us; the launch traced here: 27.8 us
  Pallas kernels  27.2 us (97%)
  between operations  0.64 us (2%)
    pallas_call x1, Pallas kernels, body(): pl.pallas_call(kernel, out_shape=outs, in_specs=[in_hbm] * 4, out_specs=(...  26.5 us
    pallas_call x1, Pallas kernels, body(): pl.pallas_call(hand_out, out_shape=tuple((pltpu.HBM(x.shape, x.dtype) for...  0.72 us

profile of v11, /device:TPU:8, one launch (start us, length us, event | category | flops | bytes accessed | tf_op | source)
XLA Modules:
  0.0 27.8 jit_solution(3602943517643615891)
XLA Ops:
  0.6 26.5 %shard_map.59 = (bf16[64,2048]{1,0:T(8,128)(2,1)S(1)}, f32[1,1,32,32]{3,2,1,0:T(8,128)S(1)}) custom-call(s32[64,64]{1,0:T(8,128)} %heights_hbm.1, s32[64,64]{1,0:T(8,128)} %blocked_hbm.1, bf16[64,2048]{1,0:T(8,128)(2,1)} %estimate_hbm.1, s32[1,1,32]{2,1,0:T(1,128)} %portal_hbm.1), custom_call_target="tpu_custom_call" | custom-call | tf_op jit(solution)/shard_map/pallas_call | solution.py:460
  27.1 0.7 %shard_map.60 = (bf16[64,2048]{1,0:T(8,128)(2,1)}, f32[1,1,32,32]{3,2,1,0:T(8,128)}) custom-call(bf16[64,2048]{1,0:T(8,128)(2,1)S(1)} %get-tuple-element.4.relaxed_in, f32[1,1,32,32]{3,2,1,0:T(8,128)S(1)} %get-tuple-element.5.merged_in), custom_call_target="tpu_custom_call" | custom-call | tf_op jit(solution)/shard_map/pallas_call | solution.py:498
